TPU v7x, 512 devices: a whole 4x8x8 slice. The times are simulated.
512 devices in a mesh: row: 32 (over z_hi, y), col: 16 (over z_lo, x, core).
Axes of the slice: x: 4, y: 8, z: 8 (z_hi: 4, z_lo: 2; z = z_hi * 2 + z_lo), core: 2. Of those that a mesh axis runs over, the one named last changes fastest.
Arguments:
- blocks: bfloat16 [32, 16, 8, 256, 256], P('row', 'col'), may hold values from -0.875 to 0.875
- block_slots: int32 [32, 16, 8], P('row', 'col'), may hold values from 0 to 8, as said below
- density: bfloat16 [16384, 16384], P('row', 'col'), may hold values from -3 to 3
- branch: int32 [64], replicated, may hold values from 0 to 1
Outputs:
- purified: float32 [16384, 16384], P('row', 'col')
Inputs may be any that keep to these rules, and one draw needn't show every extreme that they name: `block_slots`: in each tile the stored slots name distinct positions below 8; an empty slot holds 8; at least half of a tile's slots are stored.
All inputs are finite; a program needn't handle non-finite values.
Results may differ from a plain program's by a relative error of at most 0.0003.
Values may be sent and summed in bfloat16 or wider, within the bound.
No kernel may reach another device: no remote copies, remote signals or barrier semaphores. Data moves between devices by JAX's collectives and lax.ppermute only.
A program may use at most 64 MiB of HBM per device.

v0:
```python
import jax
import jax.numpy as jnp
from jax import lax
from jax.sharding import PartitionSpec as P

BLOCK = 256
ROW_SET = 4
COL_SET = 2
STEPS = 4
SLOT = 8


def partner(shard, axis, distance):
    return lax.ppermute(shard, axis, [(i, i ^ 1 << distance) for i in range(lax.axis_size(axis))])


def shifted(shard, axis, by):
    peers = lax.axis_size(axis)
    return lax.ppermute(shard, axis, [(i, (i + by) % peers) for i in range(peers)])


def build_tile(blocks_dev, slots_dev):
    onehot = (slots_dev[:, None] == jnp.arange(SLOT, dtype=jnp.int32)[None, :]).astype(jnp.bfloat16)
    onehot = onehot.reshape(SLOT, ROW_SET, COL_SET)
    placed = jnp.einsum("suq,sit->uiqt", onehot, blocks_dev, preferred_element_type=jnp.float32)
    return placed.astype(jnp.bfloat16).reshape(ROW_SET * BLOCK, COL_SET * BLOCK)


def contract(left_tile, right_tile):
    return lax.dot_general(
        left_tile, right_tile, (((1,), (1,)), ((), ())), preferred_element_type=jnp.float32
    )


def body(blocks, block_slots, density, branch):
    grid_size = lax.axis_size("col")
    row_count = lax.axis_size("row")
    layer_count = row_count // grid_size
    grid_bits = grid_size.bit_length() - 1
    layer_bits = layer_count.bit_length() - 1
    own_tile = build_tile(blocks[0, 0], block_slots[0, 0])
    tile_rows = own_tile.shape[0]
    row_place = lax.axis_index("row")
    col_place = lax.axis_index("col")
    panel_place = row_place // layer_count
    layer_place = row_place % layer_count
    crossing = jnp.bitwise_xor(panel_place, col_place)
    mirrored = own_tile
    for bit_level in range(grid_bits):
        across = partner(mirrored, "col", bit_level)
        opposite = partner(across, "row", bit_level + layer_bits)
        wanted = jnp.right_shift(crossing, bit_level) % 2 == 1
        mirrored = jnp.where(wanted, opposite, mirrored)
    summed = jnp.zeros((tile_rows, tile_rows), jnp.float32)
    left_tile = own_tile
    right_tile = mirrored
    for section_index in range(STEPS):
        if section_index > 0:
            left_tile = shifted(left_tile, "col", -1)
            right_tile = shifted(right_tile, "row", -layer_count)
        summed = summed + contract(left_tile, right_tile)
    bit_level = 0
    half_rows = summed.shape[0] // 2
    upper_half = jnp.right_shift(layer_place, bit_level) % 2
    kept = lax.dynamic_slice_in_dim(summed, upper_half * half_rows, half_rows, 0)
    given = lax.dynamic_slice_in_dim(summed, (1 - upper_half) * half_rows, half_rows, 0)
    summed = kept + partner(given, "row", bit_level)
    segment_rows = density.shape[0]
    block_count = segment_rows // BLOCK
    local_branch = lax.dynamic_slice_in_dim(branch, row_place * block_count, block_count, 0)
    row_branch = jnp.repeat(local_branch, BLOCK)
    doubled = 2.0 * density.astype(jnp.float32) - summed
    return jnp.where(row_branch[:, None] == 1, summed, doubled)


def solution(mesh):
    in_specs = (P("row", "col", None, None, None), P("row", "col", None), P("row", "col"), P())
    out_specs = P("row", "col")
    return jax.shard_map(body, mesh=mesh, in_specs=in_specs, out_specs=out_specs, check_vma=False)
```

profile of v0, /device:TPU:240, one launch (start us, length us, event | category | flops | bytes accessed | tf_op | source)
XLA Modules:
  0.0 549.2 jit_solution(4290032551994097885)
XLA Ops:
  0.0 2.1 fusion
  5.4 2.6 collective-permute-done
  8.0 4.0 collective-permute-start.1
  12.1 45.1 %collective-permute-done.1 = bf16[1024,512]{1,0:T(8,128)(2,1)S(1)} collective-permute-done((bf16[1024,512]{1,0:T(8,128)(2,1)S(1)}, bf16[1024,512]{1,0:T(8,128)(2,1)S(1)}, u32[]{:S(2)}, u32[]{:S(2)}) %collective-permute-start.1) | collective-permute-done | bytes 1048608 | tf_op jit(solution)/shard_map/ppermute | solution.py:14
  57.3 3.4 collective-permute-start.2
  60.7 23.5 %collective-permute-done.2 = bf16[1024,512]{1,0:T(8,128)(2,1)S(1)} collective-permute-done((bf16[1024,512]{1,0:T(8,128)(2,1)S(1)}, bf16[1024,512]{1,0:T(8,128)(2,1)S(1)}, u32[]{:S(2)}, u32[]{:S(2)}) %collective-permute-start.2) | collective-permute-done | bytes 1048608 | tf_op jit(solution)/shard_map/ppermute | solution.py:14
  86.1 43.5 %collective-permute-done.3 = bf16[1024,512]{1,0:T(8,128)(2,1)} collective-permute-done((bf16[1024,512]{1,0:T(8,128)(2,1)S(1)}, bf16[1024,512]{1,0:T(8,128)(2,1)}, u32[]{:S(2)}, u32[]{:S(2)}) %collective-permute-start.3) | collective-permute-done | bytes 1048608 | tf_op jit(solution)/shard_map/ppermute | solution.py:14
  131.0 4.9 collective-permute-start.4
  135.9 19.4 %collective-permute-done.4 = bf16[1024,512]{1,0:T(8,128)(2,1)S(1)} collective-permute-done((bf16[1024,512]{1,0:T(8,128)(2,1)S(1)}, bf16[1024,512]{1,0:T(8,128)(2,1)S(1)}, u32[]{:S(2)}, u32[]{:S(2)}) %collective-permute-start.4) | collective-permute-done | bytes 1048608 | tf_op jit(solution)/shard_map/ppermute | solution.py:14
  157.3 42.5 %collective-permute-done.5 = bf16[1024,512]{1,0:T(8,128)(2,1)} collective-permute-done((bf16[1024,512]{1,0:T(8,128)(2,1)S(1)}, bf16[1024,512]{1,0:T(8,128)(2,1)}, u32[]{:S(2)}, u32[]{:S(2)}) %collective-permute-start.5) | collective-permute-done | bytes 1048608 | tf_op jit(solution)/shard_map/ppermute | solution.py:14
  203.0 25.0 %collective-permute-done.6 = bf16[1024,512]{1,0:T(8,128)(2,1)S(1)} collective-permute-done((bf16[1024,512]{1,0:T(8,128)(2,1)S(1)}, bf16[1024,512]{1,0:T(8,128)(2,1)S(1)}, u32[]{:S(2)}, u32[]{:S(2)}) %collective-permute-start.6) | collective-permute-done | bytes 1048608 | tf_op jit(solution)/shard_map/ppermute | solution.py:14
  228.1 32.2 %collective-permute-start.7 = (bf16[1024,512]{1,0:T(8,128)(2,1)S(1)}, bf16[1024,512]{1,0:T(8,128)(2,1)}, u32[]{:S(2)}, u32[]{:S(2)}) collective-permute-start(bf16[1024,512]{1,0:T(8,128)(2,1)S(1)} %collective-permute-done.6), channel_id=1, source_target_pairs={{0,256},{16,272},{32,288},{48,304},{64,320},{80,336},{96,352},{112... | collective-permute-start | bytes 3145736 | tf_op jit(solution)/shard_map/ppermute | solution.py:14
  262.2 20.3 %collective-permute-done.7 = bf16[1024,512]{1,0:T(8,128)(2,1)} collective-permute-done((bf16[1024,512]{1,0:T(8,128)(2,1)S(1)}, bf16[1024,512]{1,0:T(8,128)(2,1)}, u32[]{:S(2)}, u32[]{:S(2)}) %collective-permute-start.7) | collective-permute-done | bytes 1048608 | tf_op jit(solution)/shard_map/ppermute | solution.py:14
  283.9 14.2 %collective-permute-start.9 = (bf16[1024,512]{1,0:T(8,128)(2,1)S(1)}, bf16[1024,512]{1,0:T(8,128)(2,1)S(1)}, u32[]{:S(2)}, u32[]{:S(2)}) collective-permute-start(bf16[1024,512]{1,0:T(8,128)(2,1)S(1)} %broadcast_select_fusion.3), channel_id=1, source_target_pairs={{0,480},{16,496},{32,0},{48,16},{64,32},{80,48},{96,64},{112,80},{... | collective-permute-start | bytes 3145736 | tf_op jit(solution)/shard_map/ppermute | solution.py:19
  298.1 28.5 %collective-permute-done.8 = bf16[1024,512]{1,0:T(8,128)(2,1)} collective-permute-done((bf16[1024,512]{1,0:T(8,128)(2,1)S(1)}, bf16[1024,512]{1,0:T(8,128)(2,1)}, u32[]{:S(2)}, u32[]{:S(2)}) %collective-permute-start.8) | collective-permute-done | bytes 1048608 | tf_op jit(solution)/shard_map/ppermute | solution.py:19
  326.6 6.3 %collective-permute-start.10 = (bf16[1024,512]{1,0:T(8,128)(2,1)}, bf16[1024,512]{1,0:T(8,128)(2,1)}, u32[]{:S(2)}, u32[]{:S(2)}) collective-permute-start(bf16[1024,512]{1,0:T(8,128)(2,1)} %collective-permute-done.8), channel_id=1, source_target_pairs={{0,15},{1,0},{2,1},{3,2},{4,3},{5,4},{6,5},{7,6},{8,7},{9,8},{10,9... | collective-permute-start | bytes 3145736 | tf_op jit(solution)/shard_map/ppermute | solution.py:19
  335.0 105.3 %collective-permute-done.10 = bf16[1024,512]{1,0:T(8,128)(2,1)} collective-permute-done((bf16[1024,512]{1,0:T(8,128)(2,1)}, bf16[1024,512]{1,0:T(8,128)(2,1)}, u32[]{:S(2)}, u32[]{:S(2)}) %collective-permute-start.10) | collective-permute-done | bytes 1048608 | tf_op jit(solution)/shard_map/ppermute | solution.py:19
  440.2 5.9 %collective-permute-start.12 = (bf16[1024,512]{1,0:T(8,128)(2,1)}, bf16[1024,512]{1,0:T(8,128)(2,1)S(1)}, u32[]{:S(2)}, u32[]{:S(2)}) collective-permute-start(bf16[1024,512]{1,0:T(8,128)(2,1)} %collective-permute-done.10), channel_id=1, source_target_pairs={{0,15},{1,0},{2,1},{3,2},{4,3},{5,4},{6,5},{7,6},{8,7},{9,8},{10,9... | collective-permute-start | bytes 3145736 | tf_op jit(solution)/shard_map/ppermute | solution.py:19
  449.4 2.5 fusion.8
  451.9 2.8 fusion.9
  454.7 4.1 collective-permute-done.12
  458.8 35.6 %collective-permute-done.13 = bf16[1024,512]{1,0:T(8,128)(2,1)S(1)} collective-permute-done((bf16[1024,512]{1,0:T(8,128)(2,1)}, bf16[1024,512]{1,0:T(8,128)(2,1)S(1)}, u32[]{:S(2)}, u32[]{:S(2)}) %collective-permute-start.13) | collective-permute-done | bytes 1048608 | tf_op jit(solution)/shard_map/ppermute | solution.py:19
  500.1 45.1 %collective-permute-done.14 = f32[512,1024]{1,0:T(8,128)} collective-permute-done((f32[512,1024]{1,0:T(8,128)S(1)}, f32[512,1024]{1,0:T(8,128)}, u32[]{:S(2)}, u32[]{:S(2)}) %collective-permute-start.14) | collective-permute-done | bytes 2097184 | tf_op jit(solution)/shard_map/ppermute | solution.py:14
  545.2 3.9 subtract_select_fusion
  (29 shorter events, 25.8 us)
Async XLA Ops:
  3.5 4.6 collective-permute-start
  8.0 49.2 %collective-permute-start.1 = (bf16[1024,512]{1,0:T(8,128)(2,1)S(1)}, bf16[1024,512]{1,0:T(8,128)(2,1)S(1)}, u32[]{:S(2)}, u32[]{:S(2)}) collective-permute-start(bf16[1024,512]{1,0:T(8,128)(2,1)S(1)} %collective-permute-done), channel_id=1, source_target_pairs={{0,32},{16,48},{32,0},{48,16},{64,96},{80,112},{96,64},{112,80},{1... | collective-permute-start | bytes 3145736 | tf_op jit(solution)/shard_map/ppermute | solution.py:14
  57.3 26.9 %collective-permute-start.2 = (bf16[1024,512]{1,0:T(8,128)(2,1)S(1)}, bf16[1024,512]{1,0:T(8,128)(2,1)S(1)}, u32[]{:S(2)}, u32[]{:S(2)}) collective-permute-start(bf16[1024,512]{1,0:T(8,128)(2,1)S(1)} %broadcast_select_fusion), channel_id=1, source_target_pairs={{0,2},{1,3},{2,0},{3,1},{4,6},{5,7},{6,4},{7,5},{8,10},{9,11},{10,... | collective-permute-start | bytes 3145736 | tf_op jit(solution)/shard_map/ppermute | solution.py:14
  84.2 45.5 %collective-permute-start.3 = (bf16[1024,512]{1,0:T(8,128)(2,1)S(1)}, bf16[1024,512]{1,0:T(8,128)(2,1)}, u32[]{:S(2)}, u32[]{:S(2)}) collective-permute-start(bf16[1024,512]{1,0:T(8,128)(2,1)S(1)} %collective-permute-done.2), channel_id=1, source_target_pairs={{0,64},{16,80},{32,96},{48,112},{64,0},{80,16},{96,32},{112,48},{1... | collective-permute-start | bytes 3145736 | tf_op jit(solution)/shard_map/ppermute | solution.py:14
  131.0 24.3 %collective-permute-start.4 = (bf16[1024,512]{1,0:T(8,128)(2,1)S(1)}, bf16[1024,512]{1,0:T(8,128)(2,1)S(1)}, u32[]{:S(2)}, u32[]{:S(2)}) collective-permute-start(bf16[1024,512]{1,0:T(8,128)(2,1)S(1)} %broadcast_select_fusion.1), channel_id=1, source_target_pairs={{0,4},{1,5},{2,6},{3,7},{4,0},{5,1},{6,2},{7,3},{8,12},{9,13},{10,... | collective-permute-start | bytes 3145736 | tf_op jit(solution)/shard_map/ppermute | solution.py:14
  155.3 44.4 %collective-permute-start.5 = (bf16[1024,512]{1,0:T(8,128)(2,1)S(1)}, bf16[1024,512]{1,0:T(8,128)(2,1)}, u32[]{:S(2)}, u32[]{:S(2)}) collective-permute-start(bf16[1024,512]{1,0:T(8,128)(2,1)S(1)} %collective-permute-done.4), channel_id=1, source_target_pairs={{0,128},{16,144},{32,160},{48,176},{64,192},{80,208},{96,224},{112... | collective-permute-start | bytes 3145736 | tf_op jit(solution)/shard_map/ppermute | solution.py:14
  201.1 27.0 %collective-permute-start.6 = (bf16[1024,512]{1,0:T(8,128)(2,1)S(1)}, bf16[1024,512]{1,0:T(8,128)(2,1)S(1)}, u32[]{:S(2)}, u32[]{:S(2)}) collective-permute-start(bf16[1024,512]{1,0:T(8,128)(2,1)S(1)} %broadcast_select_fusion.2), channel_id=1, source_target_pairs={{0,8},{1,9},{2,10},{3,11},{4,12},{5,13},{6,14},{7,15},{8,0},{9,1},... | collective-permute-start | bytes 3145736 | tf_op jit(solution)/shard_map/ppermute | solution.py:14
  228.1 54.5 %collective-permute-start.7 = (bf16[1024,512]{1,0:T(8,128)(2,1)S(1)}, bf16[1024,512]{1,0:T(8,128)(2,1)}, u32[]{:S(2)}, u32[]{:S(2)}) collective-permute-start(bf16[1024,512]{1,0:T(8,128)(2,1)S(1)} %collective-permute-done.6), channel_id=1, source_target_pairs={{0,256},{16,272},{32,288},{48,304},{64,320},{80,336},{96,352},{112... | collective-permute-start | bytes 3145736 | tf_op jit(solution)/shard_map/ppermute | solution.py:14
  260.3 66.3 %collective-permute-start.8 = (bf16[1024,512]{1,0:T(8,128)(2,1)S(1)}, bf16[1024,512]{1,0:T(8,128)(2,1)}, u32[]{:S(2)}, u32[]{:S(2)}) collective-permute-start(bf16[1024,512]{1,0:T(8,128)(2,1)S(1)} %bitcast.25), channel_id=1, source_target_pairs={{0,15},{1,0},{2,1},{3,2},{4,3},{5,4},{6,5},{7,6},{8,7},{9,8},{10,9... | collective-permute-start | bytes 3145736 | tf_op jit(solution)/shard_map/ppermute | solution.py:19
  283.9 49.1 %collective-permute-start.9 = (bf16[1024,512]{1,0:T(8,128)(2,1)S(1)}, bf16[1024,512]{1,0:T(8,128)(2,1)S(1)}, u32[]{:S(2)}, u32[]{:S(2)}) collective-permute-start(bf16[1024,512]{1,0:T(8,128)(2,1)S(1)} %broadcast_select_fusion.3), channel_id=1, source_target_pairs={{0,480},{16,496},{32,0},{48,16},{64,32},{80,48},{96,64},{112,80},{... | collective-permute-start | bytes 3145736 | tf_op jit(solution)/shard_map/ppermute | solution.py:19
  326.6 113.6 %collective-permute-start.10 = (bf16[1024,512]{1,0:T(8,128)(2,1)}, bf16[1024,512]{1,0:T(8,128)(2,1)}, u32[]{:S(2)}, u32[]{:S(2)}) collective-permute-start(bf16[1024,512]{1,0:T(8,128)(2,1)} %collective-permute-done.8), channel_id=1, source_target_pairs={{0,15},{1,0},{2,1},{3,2},{4,3},{5,4},{6,5},{7,6},{8,7},{9,8},{10,9... | collective-permute-start | bytes 3145736 | tf_op jit(solution)/shard_map/ppermute | solution.py:19
  333.0 113.2 %collective-permute-start.11 = (bf16[1024,512]{1,0:T(8,128)(2,1)S(1)}, bf16[1024,512]{1,0:T(8,128)(2,1)}, u32[]{:S(2)}, u32[]{:S(2)}) collective-permute-start(bf16[1024,512]{1,0:T(8,128)(2,1)S(1)} %collective-permute-done.9), channel_id=1, source_target_pairs={{0,480},{16,496},{32,0},{48,16},{64,32},{80,48},{96,64},{112,80},{... | collective-permute-start | bytes 3145736 | tf_op jit(solution)/shard_map/ppermute | solution.py:19
  440.2 18.5 %collective-permute-start.12 = (bf16[1024,512]{1,0:T(8,128)(2,1)}, bf16[1024,512]{1,0:T(8,128)(2,1)S(1)}, u32[]{:S(2)}, u32[]{:S(2)}) collective-permute-start(bf16[1024,512]{1,0:T(8,128)(2,1)} %collective-permute-done.10), channel_id=1, source_target_pairs={{0,15},{1,0},{2,1},{3,2},{4,3},{5,4},{6,5},{7,6},{8,7},{9,8},{10,9... | collective-permute-start | bytes 3145736 | tf_op jit(solution)/shard_map/ppermute | solution.py:19
  446.2 48.2 %collective-permute-start.13 = (bf16[1024,512]{1,0:T(8,128)(2,1)}, bf16[1024,512]{1,0:T(8,128)(2,1)S(1)}, u32[]{:S(2)}, u32[]{:S(2)}) collective-permute-start(bf16[1024,512]{1,0:T(8,128)(2,1)} %collective-permute-done.11), channel_id=1, source_target_pairs={{0,480},{16,496},{32,0},{48,16},{64,32},{80,48},{96,64},{112,80},{... | collective-permute-start | bytes 3145736 | tf_op jit(solution)/shard_map/ppermute | solution.py:19
  495.7 2.0 copy-start
  497.7 2.2 copy-start.2
  497.7 47.5 %copy-start.1 = (bf16[512,1024]{1,0:T(8,128)(2,1)S(1)}, bf16[512,1024]{1,0:T(8,128)(2,1)}, u32[]{:S(2)}) copy-start(bf16[512,1024]{1,0:T(8,128)(2,1)} %param.6) | copy-start | bytes 3145732
  497.8 47.4 %collective-permute-start.14 = (f32[512,1024]{1,0:T(8,128)S(1)}, f32[512,1024]{1,0:T(8,128)}, u32[]{:S(2)}, u32[]{:S(2)}) collective-permute-start(f32[512,1024]{1,0:T(8,128)S(1)} %constant_dynamic-slice_fusion), channel_id=1, source_target_pairs={{0,16},{16,0},{32,48},{48,32},{64,80},{80,64},{96,112},{112,96},{1... | collective-permute-start | bytes 6291464 | tf_op jit(solution)/shard_map/ppermute | solution.py:14
where the time goes:
time: 550 us; the launch traced here: 549 us
  waiting for transfers between devices  441 us (80%)
  starting transfers between devices  86.5 us (16%)
  matrix products  10 us (2%)
  other arithmetic  8.12 us (1%)
    ppermute x9, waiting for transfers between devices, partner(): lax.ppermute(shard, axis, [(i, i ^ 1 << distance) for i in range(lax.axis...  267 us
    ppermute x6, waiting for transfers between devices, shifted(): lax.ppermute(shard, axis, [(i, (i + by) % peers) for i in range(peers)])  173 us
    ppermute x9, starting transfers between devices, partner(): lax.ppermute(shard, axis, [(i, i ^ 1 << distance) for i in range(lax.axis...  54.3 us
    ppermute x6, starting transfers between devices, shifted(): lax.ppermute(shard, axis, [(i, (i + by) % peers) for i in range(peers)])  32.3 us
  transfers between devices with their start and end apart: 15, of which 13 were waited for; matrix products, arithmetic and copies ran while one was open for 1% of the time, Pallas kernels for 0%

commit v1 on v0

v1 whole, which is shorter than its diff:
```python
import jax
import jax.numpy as jnp
from jax import lax
from jax.sharding import PartitionSpec as P

BLOCK = 256
ROW_SET = 4
COL_SET = 2
STEPS = 4
SLOT = 8
CHUNKS = 2
LAYER_TYPE = jnp.float32


def place(flat):
    row, col = divmod(flat, 16)
    return row // 8, row % 8, col // 8, col % 8 // 2, col % 2


def index(zh, y, zl, x, core):
    return ((zh % 4) * 8 + y % 8) * 16 + zl * 8 + x * 2 + core


def move(value, where):
    pairs = [(i, where(*place(i))) for i in range(512)]
    return lax.ppermute(value, ("row", "col"), [p for p in pairs if p[1] is not None])


def along_y(value, by):
    return move(value, lambda zh, y, zl, x, core: index(zh, y + by, zl, x, core))


def mirror(value, flip):
    def where(zh, y, zl, x, core):
        return index(zl * 2 + x // 2, y, zh // 2, (zh % 2) * 2 + (x % 2 ^ flip // 2), core ^ flip % 2)

    return move(value, where)


def build_tile(blocks_dev, slots_dev):
    onehot = (slots_dev[:, None] == jnp.arange(SLOT, dtype=jnp.int32)[None, :]).astype(jnp.bfloat16)
    onehot = onehot.reshape(SLOT, ROW_SET, COL_SET)
    placed = jnp.einsum("suq,sit->uiqt", onehot, blocks_dev, preferred_element_type=jnp.float32)
    return placed.astype(jnp.bfloat16).reshape(ROW_SET * BLOCK, COL_SET * BLOCK)


def pick(stack, i):
    return lax.dynamic_index_in_dim(stack, i, 0, keepdims=False)


def body(blocks, block_slots, density, branch):
    row_place = lax.axis_index("row")
    col_place = lax.axis_index("col")
    layer = row_place % 2
    q = row_place // 2 % 4
    own = col_place % 4
    core = own % 2
    upper = own // 2
    tile = build_tile(blocks[0, 0], block_slots[0, 0])
    width = COL_SET * BLOCK
    quarters = tile.reshape(ROW_SET, BLOCK, width)
    span = BLOCK // CHUNKS
    half = span // 2

    windows = []
    for chunk in range(CHUNKS):
        part = quarters[:, chunk * span:(chunk + 1) * span]
        came = jnp.stack([mirror(pick(part, own ^ flip), flip) for flip in range(4)])
        held = jnp.stack([pick(came, own ^ j) for j in range(4)])
        following = move(held[:3], lambda zh, y, zl, x, core: index(zh - 1, y, zl, x, core))
        windows.append(jnp.concatenate([held, following]))

    near = lax.ppermute(tile, "col", [(i, i - 1) for i in range(1, 16, 2)])
    second = lax.ppermute(tile, "col", [(i, (i - 2) % 16) for i in range(16)])
    swapped = lax.ppermute(second, "col", [(i, i ^ 1) for i in range(16)])
    far = lax.ppermute(second, "col", [(i, (i - 1) % 16) for i in range(0, 16, 2)])
    first = jnp.where(core == 0, near, swapped)
    third = jnp.where(core == 0, swapped, far)
    left = jnp.concatenate([tile, first, second, third], axis=1)
    half_rows = left.shape[0] // 2
    left_kept = lax.dynamic_slice_in_dim(left, layer * half_rows, half_rows, 0)
    left_given = lax.dynamic_slice_in_dim(left, (1 - layer) * half_rows, half_rows, 0)

    outs = []
    for chunk in range(CHUNKS):
        window = windows[chunk]

        def view(shift):
            return lax.dynamic_slice_in_dim(window, (q + shift) % 4, 4, 0)

        ahead = along_y(jnp.concatenate([view(1), view(2)[:, :half]], axis=1), 2)
        back = along_y(jnp.concatenate([view(3), view(2)[:, half:]], axis=1), -2)
        ahead_two = along_y(ahead[:, span:], 2)
        back_two = along_y(back[:, span:], -2)
        mine = view(0)
        before, after = ahead[:, :span], back[:, :span]
        opposite = jnp.concatenate([ahead_two, back_two], axis=1)
        even = jnp.stack([mine, opposite])
        odd = jnp.stack([before, after])
        matches = core == q % 2
        kept = jnp.where(matches, even, odd)
        came = move(jnp.where(matches, odd, even), lambda zh, y, zl, x, core: index(zh, y, zl, x, core ^ 1))
        leading = jnp.where(matches, q, (q + 3) % 4) // 2
        chosen = jnp.where(leading == upper, 0, 1)
        stay = jnp.stack([pick(kept, chosen), pick(came, chosen)])
        leave = jnp.stack([pick(kept, 1 - chosen), pick(came, 1 - chosen)])
        other = move(leave, lambda zh, y, zl, x, core: index(zh, y, zl, x ^ 1, core))
        both = jnp.concatenate([stay, other])
        right = jnp.stack([pick(both, own ^ u) for u in range(4)])
        right = right.transpose(0, 2, 1, 3).reshape(ROW_SET * span, STEPS * width)

        def contract(rows):
            return lax.dot_general(rows, right, (((1,), (1,)), ((), ())), preferred_element_type=jnp.float32)

        given = contract(left_given).astype(LAYER_TYPE)
        received = move(given, lambda zh, y, zl, x, core: index(zh, y ^ 1, zl, x, core))
        summed = contract(left_kept) + received.astype(jnp.float32)
        outs.append(summed.reshape(half_rows, ROW_SET, span))
    summed = jnp.stack(outs, axis=2).reshape(half_rows, ROW_SET * BLOCK)
    block_count = half_rows // BLOCK
    local_branch = lax.dynamic_slice_in_dim(branch, row_place * block_count, block_count, 0)
    row_branch = jnp.repeat(local_branch, BLOCK)
    doubled = 2.0 * density.astype(jnp.float32) - summed
    return jnp.where(row_branch[:, None] == 1, summed, doubled)


def solution(mesh):
    in_specs = (P("row", "col", None, None, None), P("row", "col", None), P("row", "col"), P())
    out_specs = P("row", "col")
    return jax.shard_map(body, mesh=mesh, in_specs=in_specs, out_specs=out_specs, check_vma=False)
```

time: 550 us -> 308 us (0.56)
  waiting for transfers between devices: 441 us -> 148 us
  local copies, waits for them, and re-layouts: 3.51 us -> 25.9 us
  starting transfers between devices: 86.5 us -> 106 us
  other arithmetic: 8.12 us -> 13.7 us
    ppermute x15 -> x28, waiting for transfers between devices: 441 us -> 148 us  [the longest x24 147 us: move(): lax.ppermute(value, ('row', 'col'), [p for p in pairs if p[1] is not None])]
    ppermute x15 -> x28, starting transfers between devices: 86.5 us -> 106 us  [the longest x24 98.1 us: move(): lax.ppermute(value, ('row', 'col'), [p for p in pairs if p[1] is not None])]
    another operation x0 -> x7, local copies, waits for them, and re-layouts: none -> 7.82 us  [the longest x4 4.32 us: body(): odd = jnp.stack([before, after])]
    concatenate x0 -> x7, other arithmetic: none -> 5.75 us  [the longest x1 2.49 us: body(): left = jnp.concatenate([tile, first, second, third], axis=1)]
  transfers between devices with their start and end apart: 15 -> 28, of which waited for: 13 -> 12; matrix products, arithmetic and copies ran while one was open for 1% -> 13% of each run, Pallas kernels for 0% -> 0%
where the time goes in v1:
time: 308 us; the launch traced here: 307 us
  waiting for transfers between devices  148 us (48%)
  starting transfers between devices  106 us (34%)
  local copies, waits for them, and re-layouts  25.9 us (8%)
  other arithmetic  13.7 us (4%)
  matrix products  12.2 us (4%)
    ppermute x24, waiting for transfers between devices, move(): lax.ppermute(value, ('row', 'col'), [p for p in pairs if p[1] is not None])  147 us
    ppermute x24, starting transfers between devices, move(): lax.ppermute(value, ('row', 'col'), [p for p in pairs if p[1] is not None])  98.1 us
    dot_general x4, matrix products, contract(): lax.dot_general(rows, right, (((1,), (1,)), ((), ())), preferred_element_...  10.1 us
  transfers between devices with their start and end apart: 28, of which 12 were waited for; matrix products, arithmetic and copies ran while one was open for 13% of the time, Pallas kernels for 0%

profile of v1, /device:TPU:240, one launch (start us, length us, event | category | flops | bytes accessed | tf_op | source)
XLA Modules:
  0.0 306.8 jit_solution(14049526977908937281)
XLA Ops:
  3.2 7.4 %collective-permute-start.5 = (bf16[128,512]{1,0:T(8,128)(2,1)S(1)}, bf16[128,512]{1,0:T(8,128)(2,1)S(1)}, u32[]{:S(2)}, u32[]{:S(2)}) collective-permute-start(bf16[128,512]{1,0:T(8,128)(2,1)S(1)} %bitcast.81), channel_id=1, source_target_pairs={{0,1},{1,0},{2,3},{3,2},{4,129},{5,128},{6,131},{7,130},{8,257},{9... | collective-permute-start | bytes 393224 | tf_op jit(solution)/shard_map/ppermute | solution.py:26
  13.1 7.0 %collective-permute-start.7 = (bf16[128,512]{1,0:T(8,128)(2,1)S(1)}, bf16[128,512]{1,0:T(8,128)(2,1)}, u32[]{:S(2)}, u32[]{:S(2)}) collective-permute-start(bf16[128,512]{1,0:T(8,128)(2,1)S(1)} %bitcast.79), channel_id=1, source_target_pairs={{0,3},{1,2},{2,1},{3,0},{4,131},{5,130},{6,129},{7,128},{8,259},{9... | collective-permute-start | bytes 393224 | tf_op jit(solution)/shard_map/ppermute | solution.py:26
  26.0 8.0 %collective-permute-start.16 = (bf16[128,512]{1,0:T(8,128)(2,1)S(1)}, bf16[128,512]{1,0:T(8,128)(2,1)S(1)}, u32[]{:S(2)}, u32[]{:S(2)}) collective-permute-start(bf16[128,512]{1,0:T(8,128)(2,1)S(1)} %bitcast.85), channel_id=1, source_target_pairs={{0,0},{1,1},{2,2},{3,3},{4,128},{5,129},{6,130},{7,131},{8,256},{9... | collective-permute-start | bytes 393224 | tf_op jit(solution)/shard_map/ppermute | solution.py:26
  36.0 6.5 %collective-permute-start.18 = (bf16[128,512]{1,0:T(8,128)(2,1)S(1)}, bf16[128,512]{1,0:T(8,128)(2,1)S(1)}, u32[]{:S(2)}, u32[]{:S(2)}) collective-permute-start(bf16[128,512]{1,0:T(8,128)(2,1)S(1)} %bitcast.83), channel_id=1, source_target_pairs={{0,2},{1,3},{2,0},{3,1},{4,130},{5,131},{6,128},{7,129},{8,258},{9... | collective-permute-start | bytes 393224 | tf_op jit(solution)/shard_map/ppermute | solution.py:26
  46.5 3.1 %collective-permute-start.8 = (bf16[3,128,512]{2,1,0:T(8,128)(2,1)S(1)}, bf16[3,128,512]{2,1,0:T(8,128)(2,1)S(1)}, u32[]{:S(2)}, u32[]{:S(2)}) collective-permute-start(bf16[3,128,512]{2,1,0:T(8,128)(2,1)S(1)} %pad_maximum_fusion.16), channel_id=1, source_target_pairs={{0,384},{1,385},{2,386},{3,387},{4,388},{5,389},{6,390},{7,391},{8... | collective-permute-start | bytes 1179656 | tf_op jit(solution)/shard_map/ppermute | solution.py:26
  51.4 4.5 %collective-permute-done.18 = bf16[128,512]{1,0:T(8,128)(2,1)S(1)} collective-permute-done((bf16[128,512]{1,0:T(8,128)(2,1)S(1)}, bf16[128,512]{1,0:T(8,128)(2,1)S(1)}, u32[]{:S(2)}, u32[]{:S(2)}) %collective-permute-start.18) | collective-permute-done | bytes 131104 | tf_op jit(solution)/shard_map/ppermute | solution.py:26
  55.9 4.6 %collective-permute-done.19 = bf16[128,512]{1,0:T(8,128)(2,1)S(1)} collective-permute-done((bf16[128,512]{1,0:T(8,128)(2,1)S(1)}, bf16[128,512]{1,0:T(8,128)(2,1)S(1)}, u32[]{:S(2)}, u32[]{:S(2)}) %collective-permute-start.19) | collective-permute-done | bytes 131104 | tf_op jit(solution)/shard_map/ppermute | solution.py:26
  60.8 4.3 %collective-permute-start.20 = (bf16[3,128,512]{2,1,0:T(8,128)(2,1)S(1)}, bf16[3,128,512]{2,1,0:T(8,128)(2,1)S(1)}, u32[]{:S(2)}, u32[]{:S(2)}) collective-permute-start(bf16[3,128,512]{2,1,0:T(8,128)(2,1)S(1)} %pad_maximum_fusion.17), channel_id=1, source_target_pairs={{0,384},{1,385},{2,386},{3,387},{4,388},{5,389},{6,390},{7,391},{8... | collective-permute-start | bytes 1179656 | tf_op jit(solution)/shard_map/ppermute | solution.py:26
  65.1 30.9 %collective-permute-done.8 = bf16[3,128,512]{2,1,0:T(8,128)(2,1)S(1)} collective-permute-done((bf16[3,128,512]{2,1,0:T(8,128)(2,1)S(1)}, bf16[3,128,512]{2,1,0:T(8,128)(2,1)S(1)}, u32[]{:S(2)}, u32[]{:S(2)}) %collective-permute-start.8) | collective-permute-done | bytes 393248 | tf_op jit(solution)/shard_map/ppermute | solution.py:26
  96.2 7.2 %collective-permute-done.20 = bf16[3,128,512]{2,1,0:T(8,128)(2,1)S(1)} collective-permute-done((bf16[3,128,512]{2,1,0:T(8,128)(2,1)S(1)}, bf16[3,128,512]{2,1,0:T(8,128)(2,1)S(1)}, u32[]{:S(2)}, u32[]{:S(2)}) %collective-permute-start.20) | collective-permute-done | bytes 393248 | tf_op jit(solution)/shard_map/ppermute | solution.py:26
  108.2 4.8 %collective-permute-start.11 = (bf16[4,192,512]{2,1,0:T(8,128)(2,1)}, bf16[4,192,512]{2,1,0:T(8,128)(2,1)}, u32[]{:S(2)}, u32[]{:S(2)}) collective-permute-start(bf16[4,192,512]{2,1,0:T(8,128)(2,1)} %pad_maximum_fusion.11), channel_id=1, source_target_pairs={{0,96},{1,97},{2,98},{3,99},{4,100},{5,101},{6,102},{7,103},{8,104... | collective-permute-start | bytes 2359304 | tf_op jit(solution)/shard_map/ppermute | solution.py:26
  113.9 3.1 %collective-permute-start.21 = (bf16[4,192,512]{2,1,0:T(8,128)(2,1)}, bf16[4,192,512]{2,1,0:T(8,128)(2,1)}, u32[]{:S(2)}, u32[]{:S(2)}) collective-permute-start(bf16[4,192,512]{2,1,0:T(8,128)(2,1)} %pad_maximum_fusion.12), channel_id=1, source_target_pairs={{0,32},{1,33},{2,34},{3,35},{4,36},{5,37},{6,38},{7,39},{8,40},{9,... | collective-permute-start | bytes 2359304 | tf_op jit(solution)/shard_map/ppermute | solution.py:26
  117.1 4.0 %collective-permute-start.23 = (bf16[4,192,512]{2,1,0:T(8,128)(2,1)S(1)}, bf16[4,192,512]{2,1,0:T(8,128)(2,1)}, u32[]{:S(2)}, u32[]{:S(2)}) collective-permute-start(bf16[4,192,512]{2,1,0:T(8,128)(2,1)S(1)} %pad_maximum_fusion.13), channel_id=1, source_target_pairs={{0,96},{1,97},{2,98},{3,99},{4,100},{5,101},{6,102},{7,103},{8,104... | collective-permute-start | bytes 2359304 | tf_op jit(solution)/shard_map/ppermute | solution.py:26
  121.2 23.1 %collective-permute-done.9 = bf16[4,192,512]{2,1,0:T(8,128)(2,1)} collective-permute-done((bf16[4,192,512]{2,1,0:T(8,128)(2,1)}, bf16[4,192,512]{2,1,0:T(8,128)(2,1)}, u32[]{:S(2)}, u32[]{:S(2)}) %collective-permute-start.9) | collective-permute-done | bytes 786464 | tf_op jit(solution)/shard_map/ppermute | solution.py:26
  147.1 19.3 %collective-permute-done.11 = bf16[4,192,512]{2,1,0:T(8,128)(2,1)} collective-permute-done((bf16[4,192,512]{2,1,0:T(8,128)(2,1)}, bf16[4,192,512]{2,1,0:T(8,128)(2,1)}, u32[]{:S(2)}, u32[]{:S(2)}) %collective-permute-start.11) | collective-permute-done | bytes 786464 | tf_op jit(solution)/shard_map/ppermute | solution.py:26
  167.5 3.7 %collective-permute-start.12 = (bf16[4,64,512]{2,1,0:T(8,128)(2,1)S(1)}, bf16[4,64,512]{2,1,0:T(8,128)(2,1)S(1)}, u32[]{:S(2)}, u32[]{:S(2)}) collective-permute-start(bf16[4,64,512]{2,1,0:T(8,128)(2,1)S(1)} %slice.62), channel_id=1, source_target_pairs={{0,96},{1,97},{2,98},{3,99},{4,100},{5,101},{6,102},{7,103},{8,104... | collective-permute-start | bytes 786440 | tf_op jit(solution)/shard_map/ppermute | solution.py:26
  173.5 9.1 %collective-permute-done.21 = bf16[4,192,512]{2,1,0:T(8,128)(2,1)} collective-permute-done((bf16[4,192,512]{2,1,0:T(8,128)(2,1)}, bf16[4,192,512]{2,1,0:T(8,128)(2,1)}, u32[]{:S(2)}, u32[]{:S(2)}) %collective-permute-start.21) | collective-permute-done | bytes 786464 | tf_op jit(solution)/shard_map/ppermute | solution.py:26
  190.5 10.4 %collective-permute-start.24 = (bf16[4,64,512]{2,1,0:T(8,128)(2,1)S(1)}, bf16[4,64,512]{2,1,0:T(8,128)(2,1)S(1)}, u32[]{:S(2)}, u32[]{:S(2)}) collective-permute-start(bf16[4,64,512]{2,1,0:T(8,128)(2,1)S(1)} %slice.67), channel_id=1, source_target_pairs={{0,96},{1,97},{2,98},{3,99},{4,100},{5,101},{6,102},{7,103},{8,104... | collective-permute-start | bytes 786440 | tf_op jit(solution)/shard_map/ppermute | solution.py:26
  213.4 4.7 %collective-permute-start.14 = (bf16[2,4,128,512]{3,2,1,0:T(8,128)(2,1)S(1)}, bf16[2,4,128,512]{3,2,1,0:T(8,128)(2,1)S(1)}, u32[]{:S(2)}, u32[]{:S(2)}) collective-permute-start(bf16[2,4,128,512]{3,2,1,0:T(8,128)(2,1)S(1)} %pad_maximum_fusion.6), channel_id=1, source_target_pairs={{0,2},{1,3},{2,0},{3,1},{4,6},{5,7},{6,4},{7,5},{8,10},{9,11},{10,... | collective-permute-start | bytes 3145736 | tf_op jit(solution)/shard_map/ppermute | solution.py:26
  222.4 7.7 %collective-permute-start.26 = (bf16[2,4,128,512]{3,2,1,0:T(8,128)(2,1)S(1)}, bf16[2,4,128,512]{3,2,1,0:T(8,128)(2,1)S(1)}, u32[]{:S(2)}, u32[]{:S(2)}) collective-permute-start(bf16[2,4,128,512]{3,2,1,0:T(8,128)(2,1)S(1)} %pad_maximum_fusion.9), channel_id=1, source_target_pairs={{0,2},{1,3},{2,0},{3,1},{4,6},{5,7},{6,4},{7,5},{8,10},{9,11},{10,... | collective-permute-start | bytes 3145736 | tf_op jit(solution)/shard_map/ppermute | solution.py:26
  232.6 15.1 %collective-permute-done.14 = bf16[2,4,128,512]{3,2,1,0:T(8,128)(2,1)S(1)} collective-permute-done((bf16[2,4,128,512]{3,2,1,0:T(8,128)(2,1)S(1)}, bf16[2,4,128,512]{3,2,1,0:T(8,128)(2,1)S(1)}, u32[]{:S(2)}, u32[]{:S(2)}) %collective-permute-start.14) | collective-permute-done | bytes 1048608 | tf_op jit(solution)/shard_map/ppermute | solution.py:26
  254.7 12.6 %collective-permute-done.26 = bf16[2,4,128,512]{3,2,1,0:T(8,128)(2,1)S(1)} collective-permute-done((bf16[2,4,128,512]{3,2,1,0:T(8,128)(2,1)S(1)}, bf16[2,4,128,512]{3,2,1,0:T(8,128)(2,1)S(1)}, u32[]{:S(2)}, u32[]{:S(2)}) %collective-permute-start.26) | collective-permute-done | bytes 1048608 | tf_op jit(solution)/shard_map/ppermute | solution.py:26
  274.8 3.0 fusion.9
  277.8 19.2 %collective-permute-done.27 = f32[512,512]{0,1:T(8,128)} collective-permute-done((f32[512,512]{0,1:T(8,128)}, f32[512,512]{0,1:T(8,128)}, u32[]{:S(2)}, u32[]{:S(2)}) %collective-permute-start.27) | collective-permute-done | bytes 1048608 | tf_op jit(solution)/shard_map/ppermute | solution.py:26
  (124 shorter events, 82.7 us)
Async XLA Ops:
  3.2 22.8 %collective-permute-start.5 = (bf16[128,512]{1,0:T(8,128)(2,1)S(1)}, bf16[128,512]{1,0:T(8,128)(2,1)S(1)}, u32[]{:S(2)}, u32[]{:S(2)}) collective-permute-start(bf16[128,512]{1,0:T(8,128)(2,1)S(1)} %bitcast.81), channel_id=1, source_target_pairs={{0,1},{1,0},{2,3},{3,2},{4,129},{5,128},{6,131},{7,130},{8,257},{9... | collective-permute-start | bytes 393224 | tf_op jit(solution)/shard_map/ppermute | solution.py:26
  10.8 23.3 %collective-permute-start.6 = (bf16[128,512]{1,0:T(8,128)(2,1)S(1)}, bf16[128,512]{1,0:T(8,128)(2,1)S(1)}, u32[]{:S(2)}, u32[]{:S(2)}) collective-permute-start(bf16[128,512]{1,0:T(8,128)(2,1)S(1)} %bitcast.80), channel_id=1, source_target_pairs={{0,2},{1,3},{2,0},{3,1},{4,130},{5,131},{6,128},{7,129},{8,258},{9... | collective-permute-start | bytes 393224 | tf_op jit(solution)/shard_map/ppermute | solution.py:26
  13.1 22.9 %collective-permute-start.7 = (bf16[128,512]{1,0:T(8,128)(2,1)S(1)}, bf16[128,512]{1,0:T(8,128)(2,1)}, u32[]{:S(2)}, u32[]{:S(2)}) collective-permute-start(bf16[128,512]{1,0:T(8,128)(2,1)S(1)} %bitcast.79), channel_id=1, source_target_pairs={{0,3},{1,2},{2,1},{3,0},{4,131},{5,130},{6,129},{7,128},{8,259},{9... | collective-permute-start | bytes 393224 | tf_op jit(solution)/shard_map/ppermute | solution.py:26
  20.2 22.2 %collective-permute-start.4 = (bf16[128,512]{1,0:T(8,128)(2,1)S(1)}, bf16[128,512]{1,0:T(8,128)(2,1)}, u32[]{:S(2)}, u32[]{:S(2)}) collective-permute-start(bf16[128,512]{1,0:T(8,128)(2,1)S(1)} %bitcast.78), channel_id=1, source_target_pairs={{0,0},{1,1},{2,2},{3,3},{4,128},{5,129},{6,130},{7,131},{8,256},{9... | collective-permute-start | bytes 393224 | tf_op jit(solution)/shard_map/ppermute | solution.py:26
  23.5 148.7 %collective-permute-start.1 = (bf16[1024,512]{1,0:T(8,128)(2,1)S(1)}, bf16[1024,512]{1,0:T(8,128)(2,1)}, u32[]{:S(2)}, u32[]{:S(2)}) collective-permute-start(bf16[1024,512]{1,0:T(8,128)(2,1)S(1)} %bitcast.68), channel_id=1, source_target_pairs={{0,14},{1,15},{2,0},{3,1},{4,2},{5,3},{6,4},{7,5},{8,6},{9,7},{10,... | collective-permute-start | bytes 3145736 | tf_op jit(solution)/shard_map/ppermute | solution.py:74
  26.0 20.4 %collective-permute-start.16 = (bf16[128,512]{1,0:T(8,128)(2,1)S(1)}, bf16[128,512]{1,0:T(8,128)(2,1)S(1)}, u32[]{:S(2)}, u32[]{:S(2)}) collective-permute-start(bf16[128,512]{1,0:T(8,128)(2,1)S(1)} %bitcast.85), channel_id=1, source_target_pairs={{0,0},{1,1},{2,2},{3,3},{4,128},{5,129},{6,130},{7,131},{8,256},{9... | collective-permute-start | bytes 393224 | tf_op jit(solution)/shard_map/ppermute | solution.py:26
  36.0 19.9 %collective-permute-start.18 = (bf16[128,512]{1,0:T(8,128)(2,1)S(1)}, bf16[128,512]{1,0:T(8,128)(2,1)S(1)}, u32[]{:S(2)}, u32[]{:S(2)}) collective-permute-start(bf16[128,512]{1,0:T(8,128)(2,1)S(1)} %bitcast.83), channel_id=1, source_target_pairs={{0,2},{1,3},{2,0},{3,1},{4,130},{5,131},{6,128},{7,129},{8,258},{9... | collective-permute-start | bytes 393224 | tf_op jit(solution)/shard_map/ppermute | solution.py:26
  42.5 18.1 %collective-permute-start.19 = (bf16[128,512]{1,0:T(8,128)(2,1)S(1)}, bf16[128,512]{1,0:T(8,128)(2,1)S(1)}, u32[]{:S(2)}, u32[]{:S(2)}) collective-permute-start(bf16[128,512]{1,0:T(8,128)(2,1)S(1)} %bitcast.82), channel_id=1, source_target_pairs={{0,3},{1,2},{2,1},{3,0},{4,131},{5,130},{6,129},{7,128},{8,259},{9... | collective-permute-start | bytes 393224 | tf_op jit(solution)/shard_map/ppermute | solution.py:26
  46.5 49.5 %collective-permute-start.8 = (bf16[3,128,512]{2,1,0:T(8,128)(2,1)S(1)}, bf16[3,128,512]{2,1,0:T(8,128)(2,1)S(1)}, u32[]{:S(2)}, u32[]{:S(2)}) collective-permute-start(bf16[3,128,512]{2,1,0:T(8,128)(2,1)S(1)} %pad_maximum_fusion.16), channel_id=1, source_target_pairs={{0,384},{1,385},{2,386},{3,387},{4,388},{5,389},{6,390},{7,391},{8... | collective-permute-start | bytes 1179656 | tf_op jit(solution)/shard_map/ppermute | solution.py:26
  60.8 42.6 %collective-permute-start.20 = (bf16[3,128,512]{2,1,0:T(8,128)(2,1)S(1)}, bf16[3,128,512]{2,1,0:T(8,128)(2,1)S(1)}, u32[]{:S(2)}, u32[]{:S(2)}) collective-permute-start(bf16[3,128,512]{2,1,0:T(8,128)(2,1)S(1)} %pad_maximum_fusion.17), channel_id=1, source_target_pairs={{0,384},{1,385},{2,386},{3,387},{4,388},{5,389},{6,390},{7,391},{8... | collective-permute-start | bytes 1179656 | tf_op jit(solution)/shard_map/ppermute | solution.py:26
  105.3 38.9 %collective-permute-start.9 = (bf16[4,192,512]{2,1,0:T(8,128)(2,1)}, bf16[4,192,512]{2,1,0:T(8,128)(2,1)}, u32[]{:S(2)}, u32[]{:S(2)}) collective-permute-start(bf16[4,192,512]{2,1,0:T(8,128)(2,1)} %pad_maximum_fusion.10), channel_id=1, source_target_pairs={{0,32},{1,33},{2,34},{3,35},{4,36},{5,37},{6,38},{7,39},{8,40},{9,... | collective-permute-start | bytes 2359304 | tf_op jit(solution)/shard_map/ppermute | solution.py:26
  108.2 58.3 %collective-permute-start.11 = (bf16[4,192,512]{2,1,0:T(8,128)(2,1)}, bf16[4,192,512]{2,1,0:T(8,128)(2,1)}, u32[]{:S(2)}, u32[]{:S(2)}) collective-permute-start(bf16[4,192,512]{2,1,0:T(8,128)(2,1)} %pad_maximum_fusion.11), channel_id=1, source_target_pairs={{0,96},{1,97},{2,98},{3,99},{4,100},{5,101},{6,102},{7,103},{8,104... | collective-permute-start | bytes 2359304 | tf_op jit(solution)/shard_map/ppermute | solution.py:26
  113.9 68.6 %collective-permute-start.21 = (bf16[4,192,512]{2,1,0:T(8,128)(2,1)}, bf16[4,192,512]{2,1,0:T(8,128)(2,1)}, u32[]{:S(2)}, u32[]{:S(2)}) collective-permute-start(bf16[4,192,512]{2,1,0:T(8,128)(2,1)} %pad_maximum_fusion.12), channel_id=1, source_target_pairs={{0,32},{1,33},{2,34},{3,35},{4,36},{5,37},{6,38},{7,39},{8,40},{9,... | collective-permute-start | bytes 2359304 | tf_op jit(solution)/shard_map/ppermute | solution.py:26
  117.1 68.3 %collective-permute-start.23 = (bf16[4,192,512]{2,1,0:T(8,128)(2,1)S(1)}, bf16[4,192,512]{2,1,0:T(8,128)(2,1)}, u32[]{:S(2)}, u32[]{:S(2)}) collective-permute-start(bf16[4,192,512]{2,1,0:T(8,128)(2,1)S(1)} %pad_maximum_fusion.13), channel_id=1, source_target_pairs={{0,96},{1,97},{2,98},{3,99},{4,100},{5,101},{6,102},{7,103},{8,104... | collective-permute-start | bytes 2359304 | tf_op jit(solution)/shard_map/ppermute | solution.py:26
  145.2 45.3 %collective-permute-start.10 = (bf16[4,64,512]{2,1,0:T(8,128)(2,1)S(1)}, bf16[4,64,512]{2,1,0:T(8,128)(2,1)S(1)}, u32[]{:S(2)}, u32[]{:S(2)}) collective-permute-start(bf16[4,64,512]{2,1,0:T(8,128)(2,1)S(1)} %slice.61), channel_id=1, source_target_pairs={{0,32},{1,33},{2,34},{3,35},{4,36},{5,37},{6,38},{7,39},{8,40},{9,... | collective-permute-start | bytes 786440 | tf_op jit(solution)/shard_map/ppermute | solution.py:26
  167.5 33.5 %collective-permute-start.12 = (bf16[4,64,512]{2,1,0:T(8,128)(2,1)S(1)}, bf16[4,64,512]{2,1,0:T(8,128)(2,1)S(1)}, u32[]{:S(2)}, u32[]{:S(2)}) collective-permute-start(bf16[4,64,512]{2,1,0:T(8,128)(2,1)S(1)} %slice.62), channel_id=1, source_target_pairs={{0,96},{1,97},{2,98},{3,99},{4,100},{5,101},{6,102},{7,103},{8,104... | collective-permute-start | bytes 786440 | tf_op jit(solution)/shard_map/ppermute | solution.py:26
  172.2 46.0 %collective-permute-start = (bf16[1024,512]{1,0:T(8,128)(2,1)S(1)}, bf16[1024,512]{1,0:T(8,128)(2,1)}, u32[]{:S(2)}, u32[]{:S(2)}) collective-permute-start(bf16[1024,512]{1,0:T(8,128)(2,1)S(1)} %bitcast.69), channel_id=1, source_target_pairs={{1,0},{3,2},{5,4},{7,6},{9,8},{11,10},{13,12},{15,14},{17,16},{19,... | collective-permute-start | bytes 3145736 | tf_op jit(solution)/shard_map/ppermute | solution.py:73
  182.6 35.6 %collective-permute-start.2 = (bf16[1024,512]{1,0:T(8,128)(2,1)}, bf16[1024,512]{1,0:T(8,128)(2,1)}, u32[]{:S(2)}, u32[]{:S(2)}) collective-permute-start(bf16[1024,512]{1,0:T(8,128)(2,1)} %collective-permute-done.1), channel_id=1, source_target_pairs={{0,1},{1,0},{2,3},{3,2},{4,5},{5,4},{6,7},{7,6},{8,9},{9,8},{10,11... | collective-permute-start | bytes 3145736 | tf_op jit(solution)/shard_map/ppermute | solution.py:75
  185.5 19.8 %collective-permute-start.22 = (bf16[4,64,512]{2,1,0:T(8,128)(2,1)S(1)}, bf16[4,64,512]{2,1,0:T(8,128)(2,1)S(1)}, u32[]{:S(2)}, u32[]{:S(2)}) collective-permute-start(bf16[4,64,512]{2,1,0:T(8,128)(2,1)S(1)} %slice.66), channel_id=1, source_target_pairs={{0,32},{1,33},{2,34},{3,35},{4,36},{5,37},{6,38},{7,39},{8,40},{9,... | collective-permute-start | bytes 786440 | tf_op jit(solution)/shard_map/ppermute | solution.py:26
  190.5 18.1 %collective-permute-start.24 = (bf16[4,64,512]{2,1,0:T(8,128)(2,1)S(1)}, bf16[4,64,512]{2,1,0:T(8,128)(2,1)S(1)}, u32[]{:S(2)}, u32[]{:S(2)}) collective-permute-start(bf16[4,64,512]{2,1,0:T(8,128)(2,1)S(1)} %slice.67), channel_id=1, source_target_pairs={{0,96},{1,97},{2,98},{3,99},{4,100},{5,101},{6,102},{7,103},{8,104... | collective-permute-start | bytes 786440 | tf_op jit(solution)/shard_map/ppermute | solution.py:26
  213.4 34.2 %collective-permute-start.14 = (bf16[2,4,128,512]{3,2,1,0:T(8,128)(2,1)S(1)}, bf16[2,4,128,512]{3,2,1,0:T(8,128)(2,1)S(1)}, u32[]{:S(2)}, u32[]{:S(2)}) collective-permute-start(bf16[2,4,128,512]{3,2,1,0:T(8,128)(2,1)S(1)} %pad_maximum_fusion.6), channel_id=1, source_target_pairs={{0,2},{1,3},{2,0},{3,1},{4,6},{5,7},{6,4},{7,5},{8,10},{9,11},{10,... | collective-permute-start | bytes 3145736 | tf_op jit(solution)/shard_map/ppermute | solution.py:26
  222.4 44.9 %collective-permute-start.26 = (bf16[2,4,128,512]{3,2,1,0:T(8,128)(2,1)S(1)}, bf16[2,4,128,512]{3,2,1,0:T(8,128)(2,1)S(1)}, u32[]{:S(2)}, u32[]{:S(2)}) collective-permute-start(bf16[2,4,128,512]{3,2,1,0:T(8,128)(2,1)S(1)} %pad_maximum_fusion.9), channel_id=1, source_target_pairs={{0,2},{1,3},{2,0},{3,1},{4,6},{5,7},{6,4},{7,5},{8,10},{9,11},{10,... | collective-permute-start | bytes 3145736 | tf_op jit(solution)/shard_map/ppermute | solution.py:26
  252.8 22.0 %collective-permute-start.15 = (f32[512,512]{0,1:T(8,128)}, f32[512,512]{0,1:T(8,128)S(1)}, u32[]{:S(2)}, u32[]{:S(2)}) collective-permute-start(f32[512,512]{0,1:T(8,128)} %fusion.2), channel_id=1, source_target_pairs={{0,16},{1,17},{2,18},{3,19},{4,20},{5,21},{6,22},{7,23},{8,24},{9,... | collective-permute-start | bytes 3145736 | tf_op jit(solution)/shard_map/ppermute | solution.py:26
  272.5 24.5 %collective-permute-start.27 = (f32[512,512]{0,1:T(8,128)}, f32[512,512]{0,1:T(8,128)}, u32[]{:S(2)}, u32[]{:S(2)}) collective-permute-start(f32[512,512]{0,1:T(8,128)} %fusion), channel_id=1, source_target_pairs={{0,16},{1,17},{2,18},{3,19},{4,20},{5,21},{6,22},{7,23},{8,24},{9,... | collective-permute-start | bytes 3145736 | tf_op jit(solution)/shard_map/ppermute | solution.py:26
  (11 other events, 150.4 us)

commit v2 on v0

v2 whole, which is shorter than its diff:
```python
import jax
import jax.numpy as jnp
from jax import lax
from jax.sharding import PartitionSpec as P

BLOCK = 256
ROW_SET = 4
COL_SET = 2
STEPS = 4
SLOT = 8
SPANS = (512, 512)
LAYER_TYPE = jnp.float16


def place(flat):
    row, col = divmod(flat, 16)
    return row // 8, row % 8, col // 8, col % 8 // 2, col % 2


def index(zh, y, zl, x, core):
    return ((zh % 4) * 8 + y % 8) * 16 + zl * 8 + x * 2 + core


def move(value, where):
    pairs = [(i, where(*place(i))) for i in range(512)]
    return lax.ppermute(value, ("row", "col"), [p for p in pairs if p[1] is not None])


def mirror(zh, y, zl, x, core):
    return index(zl * 2 + x // 2, y, zh // 2, zh % 2 * 2 + x % 2, core)


def mirror_before(zh, y, zl, x, core):
    if x % 2 * 2 + core == 3:
        return None
    return index(zl * 2 + x // 2 - 1, y, zh // 2, zh % 2 * 2 + x % 2, core)


def spread(turn):
    def where(zh, y, zl, x, core):
        q, low = y // 2, x % 2 * 2 + core
        to = (q + (x % 2 + core * 2 ^ turn)) % 4
        return index(zh, to * 2 + y % 2, zl, x // 2 * 2 + q // 2, q % 2)

    return where


def build_tile(blocks_dev, slots_dev):
    onehot = (slots_dev[:, None] == jnp.arange(SLOT, dtype=jnp.int32)[None, :]).astype(jnp.bfloat16)
    onehot = onehot.reshape(SLOT, ROW_SET, COL_SET)
    placed = jnp.einsum("suq,sit->uiqt", onehot, blocks_dev, preferred_element_type=jnp.float32)
    return placed.astype(jnp.bfloat16).reshape(ROW_SET * BLOCK, COL_SET * BLOCK)


def body(blocks, block_slots, density, branch):
    row_place = lax.axis_index("row")
    col_place = lax.axis_index("col")
    layer = row_place % 2
    q = row_place // 2 % 4
    low = col_place % 4
    core = col_place % 2
    tile = build_tile(blocks[0, 0], block_slots[0, 0])
    rows = tile.shape[0]
    half = rows // 2

    parts = [tile[sum(SPANS[:k]) * BLOCK // 256:sum(SPANS[:k + 1]) * BLOCK // 256] for k in range(len(SPANS))]

    def both(part):
        return move(part, mirror), move(part, mirror_before)

    def turned(value):
        return value // 2 + value % 2 * 2

    rights = []
    held = both(parts[0])
    for chunk in range(len(parts)):
        coming = both(lax.optimization_barrier((parts[chunk + 1], held))[0]) if chunk + 1 < len(parts) else None
        for turn in range(4):
            to = (q + (turned(low) ^ turn)) % 4
            chosen = jnp.where(to <= low, *held)
            if len(rights) > 2:
                chosen, rights[-3] = lax.optimization_barrier((chosen, rights[-3]))
            rights.append(move(chosen, spread(turn)))
        held = coming

    second = lax.ppermute(tile, "col", [(i, (i - 2) % 16) for i in range(16)])
    swapped = lax.ppermute(second, "col", [(i, i ^ 1) for i in range(16)])
    beside = lax.ppermute(jnp.where(core == 1, tile, second), "col", [(i, (i - 1) % 16) for i in range(16)])
    first = jnp.where(core == 0, beside, swapped)
    third = jnp.where(core == 0, swapped, beside)
    left = jnp.stack([tile, first, second, third])
    steps = [(turned((q - low) % 4 ^ turn) - q) % 4 for turn in range(4)]

    def left_rows(place):
        return [lax.dynamic_slice(left, (s, place * half, 0), (1, half, left.shape[2]))[0] for s in steps]

    left_given = left_rows(1 - layer)
    left_kept = left_rows(layer)

    def contract(lefts, rights):
        total = None
        for a, b in zip(lefts, rights):
            term = lax.dot_general(a, b, (((1,), (1,)), ((), ())), preferred_element_type=jnp.float32)
            total = term if total is None else total + term
        return total

    outs = []
    for chunk in range(len(parts)):
        came = rights[chunk * 4:chunk * 4 + 4]
        given = contract(left_given, came).astype(LAYER_TYPE)
        received = move(given, lambda zh, y, zl, x, core: index(zh, y ^ 1, zl, x, core))
        outs.append(contract(left_kept, came) + received.astype(jnp.float32))
    summed = jnp.concatenate(outs, axis=1)
    block_count = half // BLOCK
    local_branch = lax.dynamic_slice_in_dim(branch, row_place * block_count, block_count, 0)
    row_branch = jnp.repeat(local_branch, BLOCK)
    doubled = 2.0 * density.astype(jnp.float32) - summed
    return jnp.where(row_branch[:, None] == 1, summed, doubled)


def solution(mesh):
    in_specs = (P("row", "col", None, None, None), P("row", "col", None), P("row", "col"), P())
    out_specs = P("row", "col")
    return jax.shard_map(body, mesh=mesh, in_specs=in_specs, out_specs=out_specs, check_vma=False)
```

time: 550 us -> 221 us (0.40)
  the two profiles are of different devices: /device:TPU:240 before, /device:TPU:205 now
where the time goes in v2:
time: 221 us; the launch traced here: 220 us
  waiting for transfers between devices  125 us (57%)
  starting transfers between devices  58.2 us (26%)
  matrix products  18.3 us (8%)
  other arithmetic  10.2 us (5%)
  local copies, waits for them, and re-layouts  7.41 us (3%)
    ppermute x14, waiting for transfers between devices, move(): lax.ppermute(value, ('row', 'col'), [p for p in pairs if p[1] is not None])  125 us
    ppermute x14, starting transfers between devices, move(): lax.ppermute(value, ('row', 'col'), [p for p in pairs if p[1] is not None])  52.4 us
    dot_general x16, matrix products, contract(): lax.dot_general(a, b, (((1,), (1,)), ((), ())), preferred_element_type=jn...  16.2 us
    select_n x2, other arithmetic, body(): chosen = jnp.where(to <= low, *held)  5.39 us
  transfers between devices with their start and end apart: 17, of which 8 were waited for; matrix products, arithmetic and copies ran while one was open for 13% of the time, Pallas kernels for 0%

profile of v2, /device:TPU:205, one launch (start us, length us, event | category | flops | bytes accessed | tf_op | source)
XLA Modules:
  0.0 219.9 jit_solution(9643433732101005784)
XLA Ops:
  0.0 2.1 fusion
  3.5 7.0 %collective-permute-start.3 = (bf16[512,512]{1,0:T(8,128)(2,1)S(1)}, bf16[512,512]{1,0:T(8,128)(2,1)}, u32[]{:S(2)}, u32[]{:S(2)}) collective-permute-start(bf16[512,512]{1,0:T(8,128)(2,1)S(1)} %bitcast.88), channel_id=1, source_target_pairs={{0,0},{1,1},{2,2},{3,3},{4,128},{5,129},{6,130},{7,131},{8,256},{9... | collective-permute-start | bytes 1572872 | tf_op jit(solution)/shard_map/ppermute | solution.py:26
  10.5 1.9 collective-permute-start.4
  13.8 1.9 collective-permute-start
  15.9 16.5 %collective-permute-done.3 = bf16[512,512]{1,0:T(8,128)(2,1)} collective-permute-done((bf16[512,512]{1,0:T(8,128)(2,1)S(1)}, bf16[512,512]{1,0:T(8,128)(2,1)}, u32[]{:S(2)}, u32[]{:S(2)}) %collective-permute-start.3) | collective-permute-done | bytes 524320 | tf_op jit(solution)/shard_map/ppermute | solution.py:26
  32.3 15.6 %collective-permute-done.4 = bf16[512,512]{1,0:T(8,128)(2,1)} collective-permute-done((bf16[512,512]{1,0:T(8,128)(2,1)S(1)}, bf16[512,512]{1,0:T(8,128)(2,1)}, u32[]{:S(2)}, u32[]{:S(2)}) %collective-permute-start.4) | collective-permute-done | bytes 524320 | tf_op jit(solution)/shard_map/ppermute | solution.py:26
  48.0 2.7 %broadcast_select_fusion.2 = (bf16[512,512]{1,0:T(8,128)(2,1)}, bf16[512,512]{1,0:T(8,128)(2,1)}, bf16[512,512]{1,0:T(8,128)(2,1)}, bf16[512,512]{1,0:T(8,128)(2,1)}) fusion(bf16[512,512]{1,0:T(8,128)(2,1)} %collective-permute-done.3, bf16[512,512]{1,0:T(8,128)(2,1)} %collective-permute-done.4, pred[]{:T(512)S(6)} %le.19, pred[]{:T(512)S(6)} %le.18, ...), kind=kLoop, calls=%fused_computation.54 | loop fusion | flops 1048576 | bytes 3145732 | tf_op jit(solution)/shard_map/jit(_where)/select_n | solution.py:80
  50.7 9.1 %collective-permute-start.5 = (bf16[512,512]{1,0:T(8,128)(2,1)}, bf16[512,512]{1,0:T(8,128)(2,1)S(1)}, u32[]{:S(2)}, u32[]{:S(2)}) collective-permute-start(bf16[512,512]{1,0:T(8,128)(2,1)} %get-tuple-element.31), channel_id=1, source_target_pairs={{0,0},{1,64},{2,32},{3,96},{4,4},{5,68},{6,36},{7,100},{8,8},{9,72... | collective-permute-start | bytes 1572872 | tf_op jit(solution)/shard_map/ppermute | solution.py:26
  60.4 1.9 collective-permute-start.6
  62.4 1.9 collective-permute-start.7
  64.3 4.2 %collective-permute-start.8 = (bf16[512,512]{1,0:T(8,128)(2,1)}, bf16[512,512]{1,0:T(8,128)(2,1)}, u32[]{:S(2)}, u32[]{:S(2)}) collective-permute-start(bf16[512,512]{1,0:T(8,128)(2,1)} %get-tuple-element.30), channel_id=1, source_target_pairs={{0,32},{1,96},{2,0},{3,64},{4,36},{5,100},{6,4},{7,68},{8,40},{9,1... | collective-permute-start | bytes 1572872 | tf_op jit(solution)/shard_map/ppermute | solution.py:26
  71.5 1.9 collective-permute-start.2
  73.5 11.9 %collective-permute-done.6 = bf16[512,512]{1,0:T(8,128)(2,1)} collective-permute-done((bf16[512,512]{1,0:T(8,128)(2,1)S(1)}, bf16[512,512]{1,0:T(8,128)(2,1)}, u32[]{:S(2)}, u32[]{:S(2)}) %collective-permute-start.6) | collective-permute-done | bytes 524320 | tf_op jit(solution)/shard_map/ppermute | solution.py:26
  87.3 38.5 %collective-permute-done.7 = bf16[512,512]{1,0:T(8,128)(2,1)} collective-permute-done((bf16[512,512]{1,0:T(8,128)(2,1)S(1)}, bf16[512,512]{1,0:T(8,128)(2,1)}, u32[]{:S(2)}, u32[]{:S(2)}) %collective-permute-start.7) | collective-permute-done | bytes 524320 | tf_op jit(solution)/shard_map/ppermute | solution.py:26
  127.7 2.7 %broadcast_select_fusion.3 = (bf16[512,512]{1,0:T(8,128)(2,1)}, bf16[512,512]{1,0:T(8,128)(2,1)}, bf16[512,512]{1,0:T(8,128)(2,1)}, bf16[512,512]{1,0:T(8,128)(2,1)}) fusion(bf16[512,512]{1,0:T(8,128)(2,1)} %collective-permute-done.6, bf16[512,512]{1,0:T(8,128)(2,1)} %collective-permute-done.7, pred[]{:T(512)S(6)} %le.18, pred[]{:T(512)S(6)} %le.16, ...), kind=kLoop, calls=%fused_computation.55 | loop fusion | flops 1048576 | bytes 3145732 | tf_op jit(solution)/shard_map/jit(_where)/select_n | solution.py:80
  130.4 1.9 collective-permute-start.12
  135.0 1.9 collective-permute-start.13
  137.0 23.9 %collective-permute-done.10 = bf16[512,512]{1,0:T(8,128)(2,1)} collective-permute-done((bf16[512,512]{1,0:T(8,128)(2,1)}, bf16[512,512]{1,0:T(8,128)(2,1)}, u32[]{:S(2)}, u32[]{:S(2)}) %collective-permute-start.10) | collective-permute-done | bytes 524320 | tf_op jit(solution)/shard_map/ppermute | solution.py:26
  162.8 5.3 %collective-permute-start.15 = (bf16[512,512]{1,0:T(8,128)(2,1)}, bf16[512,512]{1,0:T(8,128)(2,1)S(1)}, u32[]{:S(2)}, u32[]{:S(2)}) collective-permute-start(bf16[512,512]{1,0:T(8,128)(2,1)} %get-tuple-element.26), channel_id=1, source_target_pairs={{0,96},{1,32},{2,64},{3,0},{4,100},{5,36},{6,68},{7,4},{8,104},{9,... | collective-permute-start | bytes 1572872 | tf_op jit(solution)/shard_map/ppermute | solution.py:26
  176.6 5.5 %collective-permute-start.11 = (f16[512,512]{0,1:T(8,128)(2,1)S(1)}, f16[512,512]{0,1:T(8,128)(2,1)S(1)}, u32[]{:S(2)}, u32[]{:S(2)}) collective-permute-start(f16[512,512]{0,1:T(8,128)(2,1)S(1)} %fusion.11), channel_id=1, source_target_pairs={{0,16},{1,17},{2,18},{3,19},{4,20},{5,21},{6,22},{7,23},{8,24},{9,... | collective-permute-start | bytes 1572872 | tf_op jit(solution)/shard_map/ppermute | solution.py:26
  187.6 2.3 %collective-permute-done.15 = bf16[512,512]{1,0:T(8,128)(2,1)S(1)} collective-permute-done((bf16[512,512]{1,0:T(8,128)(2,1)}, bf16[512,512]{1,0:T(8,128)(2,1)S(1)}, u32[]{:S(2)}, u32[]{:S(2)}) %collective-permute-start.15) | collective-permute-done | bytes 524320 | tf_op jit(solution)/shard_map/ppermute | solution.py:26
  191.9 5.9 %collective-permute-start.16 = (f16[512,512]{0,1:T(8,128)(2,1)S(1)}, f16[512,512]{0,1:T(8,128)(2,1)S(1)}, u32[]{:S(2)}, u32[]{:S(2)}) collective-permute-start(f16[512,512]{0,1:T(8,128)(2,1)S(1)} %fusion.12), channel_id=1, source_target_pairs={{0,16},{1,17},{2,18},{3,19},{4,20},{5,21},{6,22},{7,23},{8,24},{9,... | collective-permute-start | bytes 1572872 | tf_op jit(solution)/shard_map/ppermute | solution.py:26
  199.3 6.9 %collective-permute-done.11 = f16[512,512]{0,1:T(8,128)(2,1)S(1)} collective-permute-done((f16[512,512]{0,1:T(8,128)(2,1)S(1)}, f16[512,512]{0,1:T(8,128)(2,1)S(1)}, u32[]{:S(2)}, u32[]{:S(2)}) %collective-permute-start.11) | collective-permute-done | bytes 524320 | tf_op jit(solution)/shard_map/ppermute | solution.py:26
  206.8 9.3 %collective-permute-done.16 = f16[512,512]{0,1:T(8,128)(2,1)S(1)} collective-permute-done((f16[512,512]{0,1:T(8,128)(2,1)S(1)}, f16[512,512]{0,1:T(8,128)(2,1)S(1)}, u32[]{:S(2)}, u32[]{:S(2)}) %collective-permute-start.16) | collective-permute-done | bytes 524320 | tf_op jit(solution)/shard_map/ppermute | solution.py:26
  (53 shorter events, 36.1 us)
Async XLA Ops:
  3.5 28.8 %collective-permute-start.3 = (bf16[512,512]{1,0:T(8,128)(2,1)S(1)}, bf16[512,512]{1,0:T(8,128)(2,1)}, u32[]{:S(2)}, u32[]{:S(2)}) collective-permute-start(bf16[512,512]{1,0:T(8,128)(2,1)S(1)} %bitcast.88), channel_id=1, source_target_pairs={{0,0},{1,1},{2,2},{3,3},{4,128},{5,129},{6,130},{7,131},{8,256},{9... | collective-permute-start | bytes 1572872 | tf_op jit(solution)/shard_map/ppermute | solution.py:26
  10.5 37.5 %collective-permute-start.4 = (bf16[512,512]{1,0:T(8,128)(2,1)S(1)}, bf16[512,512]{1,0:T(8,128)(2,1)}, u32[]{:S(2)}, u32[]{:S(2)}) collective-permute-start(bf16[512,512]{1,0:T(8,128)(2,1)S(1)} %bitcast.89), channel_id=1, source_target_pairs={{0,384},{1,385},{2,386},{4,0},{5,1},{6,2},{8,128},{9,129},{10,130}... | collective-permute-start | bytes 1572872 | tf_op jit(solution)/shard_map/ppermute | solution.py:26
  13.8 54.7 %collective-permute-start = (bf16[1024,512]{1,0:T(8,128)(2,1)S(1)}, bf16[1024,512]{1,0:T(8,128)(2,1)}, u32[]{:S(2)}, u32[]{:S(2)}) collective-permute-start(bf16[1024,512]{1,0:T(8,128)(2,1)S(1)} %bitcast.83), channel_id=1, source_target_pairs={{0,14},{1,15},{2,0},{3,1},{4,2},{5,3},{6,4},{7,5},{8,6},{9,7},{10,... | collective-permute-start | bytes 3145736 | tf_op jit(solution)/shard_map/ppermute | solution.py:86
  50.7 20.9 %collective-permute-start.5 = (bf16[512,512]{1,0:T(8,128)(2,1)}, bf16[512,512]{1,0:T(8,128)(2,1)S(1)}, u32[]{:S(2)}, u32[]{:S(2)}) collective-permute-start(bf16[512,512]{1,0:T(8,128)(2,1)} %get-tuple-element.31), channel_id=1, source_target_pairs={{0,0},{1,64},{2,32},{3,96},{4,4},{5,68},{6,36},{7,100},{8,8},{9,72... | collective-permute-start | bytes 1572872 | tf_op jit(solution)/shard_map/ppermute | solution.py:26
  60.4 25.0 %collective-permute-start.6 = (bf16[512,512]{1,0:T(8,128)(2,1)S(1)}, bf16[512,512]{1,0:T(8,128)(2,1)}, u32[]{:S(2)}, u32[]{:S(2)}) collective-permute-start(bf16[512,512]{1,0:T(8,128)(2,1)S(1)} %bitcast.90), channel_id=1, source_target_pairs={{0,0},{1,1},{2,2},{3,3},{4,128},{5,129},{6,130},{7,131},{8,256},{9... | collective-permute-start | bytes 1572872 | tf_op jit(solution)/shard_map/ppermute | solution.py:26
  62.4 63.4 %collective-permute-start.7 = (bf16[512,512]{1,0:T(8,128)(2,1)S(1)}, bf16[512,512]{1,0:T(8,128)(2,1)}, u32[]{:S(2)}, u32[]{:S(2)}) collective-permute-start(bf16[512,512]{1,0:T(8,128)(2,1)S(1)} %bitcast.91), channel_id=1, source_target_pairs={{0,384},{1,385},{2,386},{4,0},{5,1},{6,2},{8,128},{9,129},{10,130}... | collective-permute-start | bytes 1572872 | tf_op jit(solution)/shard_map/ppermute | solution.py:26
  64.3 69.0 %copy-start.2 = (s32[64]{0:T(128)S(1)}, s32[64]{0:T(128)}, u32[]{:S(2)}) copy-start(s32[64]{0:T(128)} %param.7) | copy-start | bytes 772
  64.3 66.1 %collective-permute-start.8 = (bf16[512,512]{1,0:T(8,128)(2,1)}, bf16[512,512]{1,0:T(8,128)(2,1)}, u32[]{:S(2)}, u32[]{:S(2)}) collective-permute-start(bf16[512,512]{1,0:T(8,128)(2,1)} %get-tuple-element.30), channel_id=1, source_target_pairs={{0,32},{1,96},{2,0},{3,64},{4,36},{5,100},{6,4},{7,68},{8,40},{9,1... | collective-permute-start | bytes 1572872 | tf_op jit(solution)/shard_map/ppermute | solution.py:26
  69.6 98.5 %collective-permute-start.1 = (bf16[1024,512]{1,0:T(8,128)(2,1)}, bf16[1024,512]{1,0:T(8,128)(2,1)}, u32[]{:S(2)}, u32[]{:S(2)}) collective-permute-start(bf16[1024,512]{1,0:T(8,128)(2,1)} %broadcast_select_fusion), channel_id=1, source_target_pairs={{0,15},{1,0},{2,1},{3,2},{4,3},{5,4},{6,5},{7,6},{8,7},{9,8},{10,9... | collective-permute-start | bytes 3145736 | tf_op jit(solution)/shard_map/ppermute | solution.py:88
  71.5 61.9 %copy-start = (bf16[512,512]{1,0:T(8,128)(2,1)}, bf16[512,512]{1,0:T(8,128)(2,1)S(1)}, u32[]{:S(2)}) copy-start(bf16[512,512]{1,0:T(8,128)(2,1)S(1)} %collective-permute-done.5) | copy-start | bytes 1572868
  71.5 96.6 %collective-permute-start.2 = (bf16[1024,512]{1,0:T(8,128)(2,1)}, bf16[1024,512]{1,0:T(8,128)(2,1)}, u32[]{:S(2)}, u32[]{:S(2)}) collective-permute-start(bf16[1024,512]{1,0:T(8,128)(2,1)} %collective-permute-done), channel_id=1, source_target_pairs={{0,1},{1,0},{2,3},{3,2},{4,5},{5,4},{6,7},{7,6},{8,9},{9,8},{10,11... | collective-permute-start | bytes 3145736 | tf_op jit(solution)/shard_map/ppermute | solution.py:87
  85.4 49.6 %collective-permute-start.9 = (bf16[512,512]{1,0:T(8,128)(2,1)}, bf16[512,512]{1,0:T(8,128)(2,1)}, u32[]{:S(2)}, u32[]{:S(2)}) collective-permute-start(bf16[512,512]{1,0:T(8,128)(2,1)} %get-tuple-element.29), channel_id=1, source_target_pairs={{0,64},{1,0},{2,96},{3,32},{4,68},{5,4},{6,100},{7,36},{8,72},{9,8... | collective-permute-start | bytes 1572872 | tf_op jit(solution)/shard_map/ppermute | solution.py:26
  125.8 35.1 %collective-permute-start.10 = (bf16[512,512]{1,0:T(8,128)(2,1)}, bf16[512,512]{1,0:T(8,128)(2,1)}, u32[]{:S(2)}, u32[]{:S(2)}) collective-permute-start(bf16[512,512]{1,0:T(8,128)(2,1)} %get-tuple-element.20), channel_id=1, source_target_pairs={{0,96},{1,32},{2,64},{3,0},{4,100},{5,36},{6,68},{7,4},{8,104},{9,... | collective-permute-start | bytes 1572872 | tf_op jit(solution)/shard_map/ppermute | solution.py:26
  130.4 32.4 %collective-permute-start.12 = (bf16[512,512]{1,0:T(8,128)(2,1)}, bf16[512,512]{1,0:T(8,128)(2,1)}, u32[]{:S(2)}, u32[]{:S(2)}) collective-permute-start(bf16[512,512]{1,0:T(8,128)(2,1)} %get-tuple-element.22), channel_id=1, source_target_pairs={{0,0},{1,64},{2,32},{3,96},{4,4},{5,68},{6,36},{7,100},{8,8},{9,72... | collective-permute-start | bytes 1572872 | tf_op jit(solution)/shard_map/ppermute | solution.py:26
  135.0 51.6 %collective-permute-start.13 = (bf16[512,512]{1,0:T(8,128)(2,1)}, bf16[512,512]{1,0:T(8,128)(2,1)S(1)}, u32[]{:S(2)}, u32[]{:S(2)}) collective-permute-start(bf16[512,512]{1,0:T(8,128)(2,1)} %get-tuple-element.24), channel_id=1, source_target_pairs={{0,32},{1,96},{2,0},{3,64},{4,36},{5,100},{6,4},{7,68},{8,40},{9,1... | collective-permute-start | bytes 1572872 | tf_op jit(solution)/shard_map/ppermute | solution.py:26
  160.9 26.3 %collective-permute-start.14 = (bf16[512,512]{1,0:T(8,128)(2,1)}, bf16[512,512]{1,0:T(8,128)(2,1)S(1)}, u32[]{:S(2)}, u32[]{:S(2)}) collective-permute-start(bf16[512,512]{1,0:T(8,128)(2,1)} %get-tuple-element.25), channel_id=1, source_target_pairs={{0,64},{1,0},{2,96},{3,32},{4,68},{5,4},{6,100},{7,36},{8,72},{9,8... | collective-permute-start | bytes 1572872 | tf_op jit(solution)/shard_map/ppermute | solution.py:26
  162.8 27.1 %collective-permute-start.15 = (bf16[512,512]{1,0:T(8,128)(2,1)}, bf16[512,512]{1,0:T(8,128)(2,1)S(1)}, u32[]{:S(2)}, u32[]{:S(2)}) collective-permute-start(bf16[512,512]{1,0:T(8,128)(2,1)} %get-tuple-element.26), channel_id=1, source_target_pairs={{0,96},{1,32},{2,64},{3,0},{4,100},{5,36},{6,68},{7,4},{8,104},{9,... | collective-permute-start | bytes 1572872 | tf_op jit(solution)/shard_map/ppermute | solution.py:26
  171.5 4.6 %copy-start.1 = (bf16[512,512]{1,0:T(8,128)(2,1)S(1)}, bf16[512,512]{1,0:T(8,128)(2,1)}, u32[]{:S(2)}) copy-start(bf16[512,512]{1,0:T(8,128)(2,1)} %copy-done) | copy-start | bytes 1572868
  176.6 29.6 %collective-permute-start.11 = (f16[512,512]{0,1:T(8,128)(2,1)S(1)}, f16[512,512]{0,1:T(8,128)(2,1)S(1)}, u32[]{:S(2)}, u32[]{:S(2)}) collective-permute-start(f16[512,512]{0,1:T(8,128)(2,1)S(1)} %fusion.11), channel_id=1, source_target_pairs={{0,16},{1,17},{2,18},{3,19},{4,20},{5,21},{6,22},{7,23},{8,24},{9,... | collective-permute-start | bytes 1572872 | tf_op jit(solution)/shard_map/ppermute | solution.py:26
  191.9 24.2 %collective-permute-start.16 = (f16[512,512]{0,1:T(8,128)(2,1)S(1)}, f16[512,512]{0,1:T(8,128)(2,1)S(1)}, u32[]{:S(2)}, u32[]{:S(2)}) collective-permute-start(f16[512,512]{0,1:T(8,128)(2,1)S(1)} %fusion.12), channel_id=1, source_target_pairs={{0,16},{1,17},{2,18},{3,19},{4,20},{5,21},{6,22},{7,23},{8,24},{9,... | collective-permute-start | bytes 1572872 | tf_op jit(solution)/shard_map/ppermute | solution.py:26

commit v3 on v2

--- a/solution.py
+++ b/solution.py
@@ -8,7 +8,7 @@
 COL_SET = 2
 STEPS = 4
 SLOT = 8
-SPANS = (512, 512)
+SPANS = (256, 384, 384)
 LAYER_TYPE = jnp.float16
 
 

time: 221 us -> 213 us (0.964)
  the two profiles are of different devices: /device:TPU:205 before, /device:TPU:178 now
where the time goes in v3:
time: 213 us; the launch traced here: 211 us
  starting transfers between devices  144 us (68%)
  waiting for transfers between devices  31.6 us (15%)
  matrix products  17.5 us (8%)
  other arithmetic  10.5 us (5%)
  local copies, waits for them, and re-layouts  6.94 us (3%)
    ppermute x21, starting transfers between devices, move(): lax.ppermute(value, ('row', 'col'), [p for p in pairs if p[1] is not None])  121 us
    ppermute x21, waiting for transfers between devices, move(): lax.ppermute(value, ('row', 'col'), [p for p in pairs if p[1] is not None])  31.6 us
    ppermute x1, starting transfers between devices, body(): lax.ppermute(jnp.where(core == 1, tile, second), 'col', [(i, (i - 1) % 16...  17.6 us
    dot_general x24, matrix products, contract(): lax.dot_general(a, b, (((1,), (1,)), ((), ())), preferred_element_type=jn...  15.4 us
    select_n x3, other arithmetic, body(): chosen = jnp.where(to <= low, *held)  4.43 us
  transfers between devices with their start and end apart: 24, of which 7 were waited for; matrix products, arithmetic and copies ran while one was open for 13% of the time, Pallas kernels for 0%

profile of v3, /device:TPU:178, one launch (start us, length us, event | category | flops | bytes accessed | tf_op | source)
XLA Modules:
  0.0 211.4 jit_solution(5942957627467041909)
XLA Ops:
  2.8 2.2 %collective-permute-start.3 = (bf16[256,512]{0,1:T(8,128)(2,1)S(1)}, bf16[256,512]{0,1:T(8,128)(2,1)S(1)}, u32[]{:S(2)}, u32[]{:S(2)}) collective-permute-start(bf16[256,512]{0,1:T(8,128)(2,1)S(1)} %bitcast.106), channel_id=1, source_target_pairs={{0,0},{1,1},{2,2},{3,3},{4,128},{5,129},{6,130},{7,131},{8,256},{9... | collective-permute-start | bytes 786440 | tf_op jit(solution)/shard_map/ppermute | solution.py:26
  5.1 10.4 %collective-permute-start.4 = (bf16[256,512]{0,1:T(8,128)(2,1)S(1)}, bf16[256,512]{0,1:T(8,128)(2,1)S(1)}, u32[]{:S(2)}, u32[]{:S(2)}) collective-permute-start(bf16[256,512]{0,1:T(8,128)(2,1)S(1)} %bitcast.107), channel_id=1, source_target_pairs={{0,384},{1,385},{2,386},{4,0},{5,1},{6,2},{8,128},{9,129},{10,130}... | collective-permute-start | bytes 786440 | tf_op jit(solution)/shard_map/ppermute | solution.py:26
  16.8 3.3 %collective-permute-start = (bf16[1024,512]{1,0:T(8,128)(2,1)S(1)}, bf16[1024,512]{1,0:T(8,128)(2,1)}, u32[]{:S(2)}, u32[]{:S(2)}) collective-permute-start(bf16[1024,512]{1,0:T(8,128)(2,1)S(1)} %bitcast.102), channel_id=1, source_target_pairs={{0,14},{1,15},{2,0},{3,1},{4,2},{5,3},{6,4},{7,5},{8,6},{9,7},{10,... | collective-permute-start | bytes 3145736 | tf_op jit(solution)/shard_map/ppermute | solution.py:86
  21.1 2.9 %collective-permute-start.6 = (bf16[384,512]{1,0:T(8,128)(2,1)S(1)}, bf16[384,512]{1,0:T(8,128)(2,1)}, u32[]{:S(2)}, u32[]{:S(2)}) collective-permute-start(bf16[384,512]{1,0:T(8,128)(2,1)S(1)} %get-tuple-element.26), channel_id=1, source_target_pairs={{0,0},{1,1},{2,2},{3,3},{4,128},{5,129},{6,130},{7,131},{8,256},{9... | collective-permute-start | bytes 1179656 | tf_op jit(solution)/shard_map/ppermute | solution.py:26
  24.0 16.0 %collective-permute-start.7 = (bf16[384,512]{1,0:T(8,128)(2,1)S(1)}, bf16[384,512]{1,0:T(8,128)(2,1)}, u32[]{:S(2)}, u32[]{:S(2)}) collective-permute-start(bf16[384,512]{1,0:T(8,128)(2,1)S(1)} %get-tuple-element.26), channel_id=1, source_target_pairs={{0,384},{1,385},{2,386},{4,0},{5,1},{6,2},{8,128},{9,129},{10,130}... | collective-permute-start | bytes 1179656 | tf_op jit(solution)/shard_map/ppermute | solution.py:26
  44.9 5.6 %collective-permute-done.5 = bf16[256,512]{0,1:T(8,128)(2,1)S(1)} collective-permute-done((bf16[256,512]{0,1:T(8,128)(2,1)}, bf16[256,512]{0,1:T(8,128)(2,1)S(1)}, u32[]{:S(2)}, u32[]{:S(2)}) %collective-permute-start.5) | collective-permute-done | bytes 262176 | tf_op jit(solution)/shard_map/ppermute | solution.py:26
  50.6 6.3 %collective-permute-start.9 = (bf16[256,512]{0,1:T(8,128)(2,1)}, bf16[256,512]{0,1:T(8,128)(2,1)S(1)}, u32[]{:S(2)}, u32[]{:S(2)}) collective-permute-start(bf16[256,512]{0,1:T(8,128)(2,1)} %get-tuple-element.58), channel_id=1, source_target_pairs={{0,64},{1,0},{2,96},{3,32},{4,68},{5,4},{6,100},{7,36},{8,72},{9,8... | collective-permute-start | bytes 786440 | tf_op jit(solution)/shard_map/ppermute | solution.py:26
  56.9 8.7 %collective-permute-start.10 = (bf16[256,512]{0,1:T(8,128)(2,1)}, bf16[256,512]{0,1:T(8,128)(2,1)S(1)}, u32[]{:S(2)}, u32[]{:S(2)}) collective-permute-start(bf16[256,512]{0,1:T(8,128)(2,1)} %get-tuple-element.29), channel_id=1, source_target_pairs={{0,96},{1,32},{2,64},{3,0},{4,100},{5,36},{6,68},{7,4},{8,104},{9,... | collective-permute-start | bytes 786440 | tf_op jit(solution)/shard_map/ppermute | solution.py:26
  69.6 4.6 %collective-permute-start.14 = (bf16[384,512]{1,0:T(8,128)(2,1)}, bf16[384,512]{1,0:T(8,128)(2,1)S(1)}, u32[]{:S(2)}, u32[]{:S(2)}) collective-permute-start(bf16[384,512]{1,0:T(8,128)(2,1)} %get-tuple-element.33), channel_id=1, source_target_pairs={{0,384},{1,385},{2,386},{4,0},{5,1},{6,2},{8,128},{9,129},{10,130}... | collective-permute-start | bytes 1179656 | tf_op jit(solution)/shard_map/ppermute | solution.py:26
  74.2 6.6 %collective-permute-start.12 = (bf16[384,512]{1,0:T(8,128)(2,1)S(1)}, bf16[384,512]{1,0:T(8,128)(2,1)S(1)}, u32[]{:S(2)}, u32[]{:S(2)}) collective-permute-start(bf16[384,512]{1,0:T(8,128)(2,1)S(1)} %get-tuple-element.31), channel_id=1, source_target_pairs={{0,0},{1,64},{2,32},{3,96},{4,4},{5,68},{6,36},{7,100},{8,8},{9,72... | collective-permute-start | bytes 1179656 | tf_op jit(solution)/shard_map/ppermute | solution.py:26
  80.8 2.3 %broadcast_select_fusion = bf16[1024,512]{1,0:T(8,128)(2,1)} fusion(bf16[1024,512]{1,0:T(8,128)(2,1)S(1)} %bitcast.104, bf16[1024,512]{1,0:T(8,128)(2,1)} %collective-permute-done, pred[]{:T(512)S(6)} %eq.100), kind=kLoop, calls=%fused_computation.32 | loop fusion | flops 524288 | bytes 3145729 | tf_op jit(solution)/shard_map/jit(_where)/select_n | solution.py:88
  83.1 17.6 %collective-permute-start.1 = (bf16[1024,512]{1,0:T(8,128)(2,1)}, bf16[1024,512]{1,0:T(8,128)(2,1)}, u32[]{:S(2)}, u32[]{:S(2)}) collective-permute-start(bf16[1024,512]{1,0:T(8,128)(2,1)} %broadcast_select_fusion), channel_id=1, source_target_pairs={{0,15},{1,0},{2,1},{3,2},{4,3},{5,4},{6,5},{7,6},{8,7},{9,8},{10,9... | collective-permute-start | bytes 3145736 | tf_op jit(solution)/shard_map/ppermute | solution.py:88
  102.7 4.7 %collective-permute-start.15 = (bf16[384,512]{1,0:T(8,128)(2,1)S(1)}, bf16[384,512]{1,0:T(8,128)(2,1)S(1)}, u32[]{:S(2)}, u32[]{:S(2)}) collective-permute-start(bf16[384,512]{1,0:T(8,128)(2,1)S(1)} %get-tuple-element.34), channel_id=1, source_target_pairs={{0,32},{1,96},{2,0},{3,64},{4,36},{5,100},{6,4},{7,68},{8,40},{9,1... | collective-permute-start | bytes 1179656 | tf_op jit(solution)/shard_map/ppermute | solution.py:26
  107.4 10.3 %collective-permute-start.16 = (bf16[384,512]{1,0:T(8,128)(2,1)}, bf16[384,512]{1,0:T(8,128)(2,1)}, u32[]{:S(2)}, u32[]{:S(2)}) collective-permute-start(bf16[384,512]{1,0:T(8,128)(2,1)} %get-tuple-element.36), channel_id=1, source_target_pairs={{0,64},{1,0},{2,96},{3,32},{4,68},{5,4},{6,100},{7,36},{8,72},{9,8... | collective-permute-start | bytes 1179656 | tf_op jit(solution)/shard_map/ppermute | solution.py:26
  117.7 2.9 %collective-permute-start.17 = (bf16[384,512]{1,0:T(8,128)(2,1)}, bf16[384,512]{1,0:T(8,128)(2,1)}, u32[]{:S(2)}, u32[]{:S(2)}) collective-permute-start(bf16[384,512]{1,0:T(8,128)(2,1)} %get-tuple-element.38), channel_id=1, source_target_pairs={{0,96},{1,32},{2,64},{3,0},{4,100},{5,36},{6,68},{7,4},{8,104},{9,... | collective-permute-start | bytes 1179656 | tf_op jit(solution)/shard_map/ppermute | solution.py:26
  121.9 7.9 %collective-permute-done.15 = bf16[384,512]{1,0:T(8,128)(2,1)S(1)} collective-permute-done((bf16[384,512]{1,0:T(8,128)(2,1)S(1)}, bf16[384,512]{1,0:T(8,128)(2,1)S(1)}, u32[]{:S(2)}, u32[]{:S(2)}) %collective-permute-start.15) | collective-permute-done | bytes 393248 | tf_op jit(solution)/shard_map/ppermute | solution.py:26
  134.4 2.3 %collective-permute-done.16 = bf16[384,512]{1,0:T(8,128)(2,1)} collective-permute-done((bf16[384,512]{1,0:T(8,128)(2,1)}, bf16[384,512]{1,0:T(8,128)(2,1)}, u32[]{:S(2)}, u32[]{:S(2)}) %collective-permute-start.16) | collective-permute-done | bytes 393248 | tf_op jit(solution)/shard_map/ppermute | solution.py:26
  136.8 2.8 %collective-permute-start.20 = (bf16[384,512]{1,0:T(8,128)(2,1)}, bf16[384,512]{1,0:T(8,128)(2,1)S(1)}, u32[]{:S(2)}, u32[]{:S(2)}) collective-permute-start(bf16[384,512]{1,0:T(8,128)(2,1)} %get-tuple-element.42), channel_id=1, source_target_pairs={{0,32},{1,96},{2,0},{3,64},{4,36},{5,100},{6,4},{7,68},{8,40},{9,1... | collective-permute-start | bytes 1179656 | tf_op jit(solution)/shard_map/ppermute | solution.py:26
  139.5 3.6 %collective-permute-done.17 = bf16[384,512]{1,0:T(8,128)(2,1)} collective-permute-done((bf16[384,512]{1,0:T(8,128)(2,1)}, bf16[384,512]{1,0:T(8,128)(2,1)}, u32[]{:S(2)}, u32[]{:S(2)}) %collective-permute-start.17) | collective-permute-done | bytes 393248 | tf_op jit(solution)/shard_map/ppermute | solution.py:26
  143.1 16.8 %collective-permute-start.21 = (bf16[384,512]{1,0:T(8,128)(2,1)}, bf16[384,512]{1,0:T(8,128)(2,1)S(1)}, u32[]{:S(2)}, u32[]{:S(2)}) collective-permute-start(bf16[384,512]{1,0:T(8,128)(2,1)} %get-tuple-element.43), channel_id=1, source_target_pairs={{0,64},{1,0},{2,96},{3,32},{4,68},{5,4},{6,100},{7,36},{8,72},{9,8... | collective-permute-start | bytes 1179656 | tf_op jit(solution)/shard_map/ppermute | solution.py:26
  166.6 10.2 %collective-permute-start.11 = (f16[512,256]{0,1:T(8,128)(2,1)S(1)}, f16[512,256]{0,1:T(8,128)(2,1)S(1)}, u32[]{:S(2)}, u32[]{:S(2)}) collective-permute-start(f16[512,256]{0,1:T(8,128)(2,1)S(1)} %fusion.18), channel_id=1, source_target_pairs={{0,16},{1,17},{2,18},{3,19},{4,20},{5,21},{6,22},{7,23},{8,24},{9,... | collective-permute-start | bytes 786440 | tf_op jit(solution)/shard_map/ppermute | solution.py:26
  188.7 4.1 %collective-permute-start.23 = (f16[512,384]{0,1:T(8,128)(2,1)S(1)}, f16[512,384]{0,1:T(8,128)(2,1)S(1)}, u32[]{:S(2)}, u32[]{:S(2)}) collective-permute-start(f16[512,384]{0,1:T(8,128)(2,1)S(1)} %fusion.11), channel_id=1, source_target_pairs={{0,16},{1,17},{2,18},{3,19},{4,20},{5,21},{6,22},{7,23},{8,24},{9,... | collective-permute-start | bytes 1179656 | tf_op jit(solution)/shard_map/ppermute | solution.py:26
  195.4 8.0 %collective-permute-done.18 = f16[512,384]{0,1:T(8,128)(2,1)S(1)} collective-permute-done((f16[512,384]{0,1:T(8,128)(2,1)S(1)}, f16[512,384]{0,1:T(8,128)(2,1)S(1)}, u32[]{:S(2)}, u32[]{:S(2)}) %collective-permute-start.18) | collective-permute-done | bytes 393248 | tf_op jit(solution)/shard_map/ppermute | solution.py:26
  203.9 3.9 %collective-permute-done.23 = f16[512,384]{0,1:T(8,128)(2,1)S(1)} collective-permute-done((f16[512,384]{0,1:T(8,128)(2,1)S(1)}, f16[512,384]{0,1:T(8,128)(2,1)S(1)}, u32[]{:S(2)}, u32[]{:S(2)}) %collective-permute-start.23) | collective-permute-done | bytes 393248 | tf_op jit(solution)/shard_map/ppermute | solution.py:26
  (78 shorter events, 46.3 us)
Async XLA Ops:
  2.8 18.2 %collective-permute-start.3 = (bf16[256,512]{0,1:T(8,128)(2,1)S(1)}, bf16[256,512]{0,1:T(8,128)(2,1)S(1)}, u32[]{:S(2)}, u32[]{:S(2)}) collective-permute-start(bf16[256,512]{0,1:T(8,128)(2,1)S(1)} %bitcast.106), channel_id=1, source_target_pairs={{0,0},{1,1},{2,2},{3,3},{4,128},{5,129},{6,130},{7,131},{8,256},{9... | collective-permute-start | bytes 786440 | tf_op jit(solution)/shard_map/ppermute | solution.py:26
  5.1 16.0 %collective-permute-start.4 = (bf16[256,512]{0,1:T(8,128)(2,1)S(1)}, bf16[256,512]{0,1:T(8,128)(2,1)S(1)}, u32[]{:S(2)}, u32[]{:S(2)}) collective-permute-start(bf16[256,512]{0,1:T(8,128)(2,1)S(1)} %bitcast.107), channel_id=1, source_target_pairs={{0,384},{1,385},{2,386},{4,0},{5,1},{6,2},{8,128},{9,129},{10,130}... | collective-permute-start | bytes 786440 | tf_op jit(solution)/shard_map/ppermute | solution.py:26
  16.8 57.4 %collective-permute-start = (bf16[1024,512]{1,0:T(8,128)(2,1)S(1)}, bf16[1024,512]{1,0:T(8,128)(2,1)}, u32[]{:S(2)}, u32[]{:S(2)}) collective-permute-start(bf16[1024,512]{1,0:T(8,128)(2,1)S(1)} %bitcast.102), channel_id=1, source_target_pairs={{0,14},{1,15},{2,0},{3,1},{4,2},{5,3},{6,4},{7,5},{8,6},{9,7},{10,... | collective-permute-start | bytes 3145736 | tf_op jit(solution)/shard_map/ppermute | solution.py:86
  21.1 35.8 %collective-permute-start.6 = (bf16[384,512]{1,0:T(8,128)(2,1)S(1)}, bf16[384,512]{1,0:T(8,128)(2,1)}, u32[]{:S(2)}, u32[]{:S(2)}) collective-permute-start(bf16[384,512]{1,0:T(8,128)(2,1)S(1)} %get-tuple-element.26), channel_id=1, source_target_pairs={{0,0},{1,1},{2,2},{3,3},{4,128},{5,129},{6,130},{7,131},{8,256},{9... | collective-permute-start | bytes 1179656 | tf_op jit(solution)/shard_map/ppermute | solution.py:26
  24.0 41.6 %collective-permute-start.7 = (bf16[384,512]{1,0:T(8,128)(2,1)S(1)}, bf16[384,512]{1,0:T(8,128)(2,1)}, u32[]{:S(2)}, u32[]{:S(2)}) collective-permute-start(bf16[384,512]{1,0:T(8,128)(2,1)S(1)} %get-tuple-element.26), channel_id=1, source_target_pairs={{0,384},{1,385},{2,386},{4,0},{5,1},{6,2},{8,128},{9,129},{10,130}... | collective-permute-start | bytes 1179656 | tf_op jit(solution)/shard_map/ppermute | solution.py:26
  41.1 9.5 %collective-permute-start.5 = (bf16[256,512]{0,1:T(8,128)(2,1)}, bf16[256,512]{0,1:T(8,128)(2,1)S(1)}, u32[]{:S(2)}, u32[]{:S(2)}) collective-permute-start(bf16[256,512]{0,1:T(8,128)(2,1)} %get-tuple-element.57), channel_id=1, source_target_pairs={{0,0},{1,64},{2,32},{3,96},{4,4},{5,68},{6,36},{7,100},{8,8},{9,72... | collective-permute-start | bytes 786440 | tf_op jit(solution)/shard_map/ppermute | solution.py:26
  43.0 26.6 %collective-permute-start.8 = (bf16[256,512]{0,1:T(8,128)(2,1)}, bf16[256,512]{0,1:T(8,128)(2,1)S(1)}, u32[]{:S(2)}, u32[]{:S(2)}) collective-permute-start(bf16[256,512]{0,1:T(8,128)(2,1)} %get-tuple-element.59), channel_id=1, source_target_pairs={{0,32},{1,96},{2,0},{3,64},{4,36},{5,100},{6,4},{7,68},{8,40},{9,1... | collective-permute-start | bytes 786440 | tf_op jit(solution)/shard_map/ppermute | solution.py:26
  50.6 32.5 %collective-permute-start.9 = (bf16[256,512]{0,1:T(8,128)(2,1)}, bf16[256,512]{0,1:T(8,128)(2,1)S(1)}, u32[]{:S(2)}, u32[]{:S(2)}) collective-permute-start(bf16[256,512]{0,1:T(8,128)(2,1)} %get-tuple-element.58), channel_id=1, source_target_pairs={{0,64},{1,0},{2,96},{3,32},{4,68},{5,4},{6,100},{7,36},{8,72},{9,8... | collective-permute-start | bytes 786440 | tf_op jit(solution)/shard_map/ppermute | solution.py:26
  56.9 43.9 %collective-permute-start.10 = (bf16[256,512]{0,1:T(8,128)(2,1)}, bf16[256,512]{0,1:T(8,128)(2,1)S(1)}, u32[]{:S(2)}, u32[]{:S(2)}) collective-permute-start(bf16[256,512]{0,1:T(8,128)(2,1)} %get-tuple-element.29), channel_id=1, source_target_pairs={{0,96},{1,32},{2,64},{3,0},{4,100},{5,36},{6,68},{7,4},{8,104},{9,... | collective-permute-start | bytes 786440 | tf_op jit(solution)/shard_map/ppermute | solution.py:26
  65.6 41.8 %collective-permute-start.13 = (bf16[384,512]{1,0:T(8,128)(2,1)}, bf16[384,512]{1,0:T(8,128)(2,1)S(1)}, u32[]{:S(2)}, u32[]{:S(2)}) collective-permute-start(bf16[384,512]{1,0:T(8,128)(2,1)} %get-tuple-element.33), channel_id=1, source_target_pairs={{0,0},{1,1},{2,2},{3,3},{4,128},{5,129},{6,130},{7,131},{8,256},{9... | collective-permute-start | bytes 1179656 | tf_op jit(solution)/shard_map/ppermute | solution.py:26
  69.6 48.1 %collective-permute-start.14 = (bf16[384,512]{1,0:T(8,128)(2,1)}, bf16[384,512]{1,0:T(8,128)(2,1)S(1)}, u32[]{:S(2)}, u32[]{:S(2)}) collective-permute-start(bf16[384,512]{1,0:T(8,128)(2,1)} %get-tuple-element.33), channel_id=1, source_target_pairs={{0,384},{1,385},{2,386},{4,0},{5,1},{6,2},{8,128},{9,129},{10,130}... | collective-permute-start | bytes 1179656 | tf_op jit(solution)/shard_map/ppermute | solution.py:26
  74.2 28.5 %collective-permute-start.12 = (bf16[384,512]{1,0:T(8,128)(2,1)S(1)}, bf16[384,512]{1,0:T(8,128)(2,1)S(1)}, u32[]{:S(2)}, u32[]{:S(2)}) collective-permute-start(bf16[384,512]{1,0:T(8,128)(2,1)S(1)} %get-tuple-element.31), channel_id=1, source_target_pairs={{0,0},{1,64},{2,32},{3,96},{4,4},{5,68},{6,36},{7,100},{8,8},{9,72... | collective-permute-start | bytes 1179656 | tf_op jit(solution)/shard_map/ppermute | solution.py:26
  83.1 78.7 %collective-permute-start.1 = (bf16[1024,512]{1,0:T(8,128)(2,1)}, bf16[1024,512]{1,0:T(8,128)(2,1)}, u32[]{:S(2)}, u32[]{:S(2)}) collective-permute-start(bf16[1024,512]{1,0:T(8,128)(2,1)} %broadcast_select_fusion), channel_id=1, source_target_pairs={{0,15},{1,0},{2,1},{3,2},{4,3},{5,4},{6,5},{7,6},{8,7},{9,8},{10,9... | collective-permute-start | bytes 3145736 | tf_op jit(solution)/shard_map/ppermute | solution.py:88
  100.8 61.1 %collective-permute-start.2 = (bf16[1024,512]{1,0:T(8,128)(2,1)}, bf16[1024,512]{1,0:T(8,128)(2,1)}, u32[]{:S(2)}, u32[]{:S(2)}) collective-permute-start(bf16[1024,512]{1,0:T(8,128)(2,1)} %collective-permute-done), channel_id=1, source_target_pairs={{0,1},{1,0},{2,3},{3,2},{4,5},{5,4},{6,7},{7,6},{8,9},{9,8},{10,11... | collective-permute-start | bytes 3145736 | tf_op jit(solution)/shard_map/ppermute | solution.py:87
  102.7 27.1 %collective-permute-start.15 = (bf16[384,512]{1,0:T(8,128)(2,1)S(1)}, bf16[384,512]{1,0:T(8,128)(2,1)S(1)}, u32[]{:S(2)}, u32[]{:S(2)}) collective-permute-start(bf16[384,512]{1,0:T(8,128)(2,1)S(1)} %get-tuple-element.34), channel_id=1, source_target_pairs={{0,32},{1,96},{2,0},{3,64},{4,36},{5,100},{6,4},{7,68},{8,40},{9,1... | collective-permute-start | bytes 1179656 | tf_op jit(solution)/shard_map/ppermute | solution.py:26
  107.4 29.3 %collective-permute-start.16 = (bf16[384,512]{1,0:T(8,128)(2,1)}, bf16[384,512]{1,0:T(8,128)(2,1)}, u32[]{:S(2)}, u32[]{:S(2)}) collective-permute-start(bf16[384,512]{1,0:T(8,128)(2,1)} %get-tuple-element.36), channel_id=1, source_target_pairs={{0,64},{1,0},{2,96},{3,32},{4,68},{5,4},{6,100},{7,36},{8,72},{9,8... | collective-permute-start | bytes 1179656 | tf_op jit(solution)/shard_map/ppermute | solution.py:26
  117.7 25.4 %collective-permute-start.17 = (bf16[384,512]{1,0:T(8,128)(2,1)}, bf16[384,512]{1,0:T(8,128)(2,1)}, u32[]{:S(2)}, u32[]{:S(2)}) collective-permute-start(bf16[384,512]{1,0:T(8,128)(2,1)} %get-tuple-element.38), channel_id=1, source_target_pairs={{0,96},{1,32},{2,64},{3,0},{4,100},{5,36},{6,68},{7,4},{8,104},{9,... | collective-permute-start | bytes 1179656 | tf_op jit(solution)/shard_map/ppermute | solution.py:26
  129.8 30.1 %collective-permute-start.19 = (bf16[384,512]{1,0:T(8,128)(2,1)}, bf16[384,512]{1,0:T(8,128)(2,1)}, u32[]{:S(2)}, u32[]{:S(2)}) collective-permute-start(bf16[384,512]{1,0:T(8,128)(2,1)} %get-tuple-element.40), channel_id=1, source_target_pairs={{0,0},{1,64},{2,32},{3,96},{4,4},{5,68},{6,36},{7,100},{8,8},{9,72... | collective-permute-start | bytes 1179656 | tf_op jit(solution)/shard_map/ppermute | solution.py:26
  136.8 48.9 %collective-permute-start.20 = (bf16[384,512]{1,0:T(8,128)(2,1)}, bf16[384,512]{1,0:T(8,128)(2,1)S(1)}, u32[]{:S(2)}, u32[]{:S(2)}) collective-permute-start(bf16[384,512]{1,0:T(8,128)(2,1)} %get-tuple-element.42), channel_id=1, source_target_pairs={{0,32},{1,96},{2,0},{3,64},{4,36},{5,100},{6,4},{7,68},{8,40},{9,1... | collective-permute-start | bytes 1179656 | tf_op jit(solution)/shard_map/ppermute | solution.py:26
  143.1 43.3 %collective-permute-start.21 = (bf16[384,512]{1,0:T(8,128)(2,1)}, bf16[384,512]{1,0:T(8,128)(2,1)S(1)}, u32[]{:S(2)}, u32[]{:S(2)}) collective-permute-start(bf16[384,512]{1,0:T(8,128)(2,1)} %get-tuple-element.43), channel_id=1, source_target_pairs={{0,64},{1,0},{2,96},{3,32},{4,68},{5,4},{6,100},{7,36},{8,72},{9,8... | collective-permute-start | bytes 1179656 | tf_op jit(solution)/shard_map/ppermute | solution.py:26
  159.9 27.0 %collective-permute-start.22 = (bf16[384,512]{1,0:T(8,128)(2,1)}, bf16[384,512]{1,0:T(8,128)(2,1)S(1)}, u32[]{:S(2)}, u32[]{:S(2)}) collective-permute-start(bf16[384,512]{1,0:T(8,128)(2,1)} %get-tuple-element.44), channel_id=1, source_target_pairs={{0,96},{1,32},{2,64},{3,0},{4,100},{5,36},{6,68},{7,4},{8,104},{9,... | collective-permute-start | bytes 1179656 | tf_op jit(solution)/shard_map/ppermute | solution.py:26
  166.6 28.4 %collective-permute-start.11 = (f16[512,256]{0,1:T(8,128)(2,1)S(1)}, f16[512,256]{0,1:T(8,128)(2,1)S(1)}, u32[]{:S(2)}, u32[]{:S(2)}) collective-permute-start(f16[512,256]{0,1:T(8,128)(2,1)S(1)} %fusion.18), channel_id=1, source_target_pairs={{0,16},{1,17},{2,18},{3,19},{4,20},{5,21},{6,22},{7,23},{8,24},{9,... | collective-permute-start | bytes 786440 | tf_op jit(solution)/shard_map/ppermute | solution.py:26
  180.5 22.9 %collective-permute-start.18 = (f16[512,384]{0,1:T(8,128)(2,1)S(1)}, f16[512,384]{0,1:T(8,128)(2,1)S(1)}, u32[]{:S(2)}, u32[]{:S(2)}) collective-permute-start(f16[512,384]{0,1:T(8,128)(2,1)S(1)} %fusion.12), channel_id=1, source_target_pairs={{0,16},{1,17},{2,18},{3,19},{4,20},{5,21},{6,22},{7,23},{8,24},{9,... | collective-permute-start | bytes 1179656 | tf_op jit(solution)/shard_map/ppermute | solution.py:26
  188.7 19.1 %collective-permute-start.23 = (f16[512,384]{0,1:T(8,128)(2,1)S(1)}, f16[512,384]{0,1:T(8,128)(2,1)S(1)}, u32[]{:S(2)}, u32[]{:S(2)}) collective-permute-start(f16[512,384]{0,1:T(8,128)(2,1)S(1)} %fusion.11), channel_id=1, source_target_pairs={{0,16},{1,17},{2,18},{3,19},{4,20},{5,21},{6,22},{7,23},{8,24},{9,... | collective-permute-start | bytes 1179656 | tf_op jit(solution)/shard_map/ppermute | solution.py:26
  (5 other events, 161.5 us)

commit v4 on v3

--- a/solution.py
+++ b/solution.py
@@ -104,18 +104,20 @@
             total = term if total is None else total + term
         return total
 
-    outs = []
+    block_count = half // BLOCK
+    local_branch = lax.dynamic_slice_in_dim(branch, row_place * block_count, block_count, 0)
+    row_branch = jnp.repeat(local_branch, BLOCK)[:, None] == 1
+    outs, begin = [], 0
     for chunk in range(len(parts)):
         came = rights[chunk * 4:chunk * 4 + 4]
         given = contract(left_given, came).astype(LAYER_TYPE)
         received = move(given, lambda zh, y, zl, x, core: index(zh, y ^ 1, zl, x, core))
-        outs.append(contract(left_kept, came) + received.astype(jnp.float32))
-    summed = jnp.concatenate(outs, axis=1)
-    block_count = half // BLOCK
-    local_branch = lax.dynamic_slice_in_dim(branch, row_place * block_count, block_count, 0)
-    row_branch = jnp.repeat(local_branch, BLOCK)
-    doubled = 2.0 * density.astype(jnp.float32) - summed
-    return jnp.where(row_branch[:, None] == 1, summed, doubled)
+        summed = contract(left_kept, came) + received.astype(jnp.float32)
+        end = begin + summed.shape[1]
+        doubled = 2.0 * density[:, begin:end].astype(jnp.float32) - summed
+        outs.append(jnp.where(row_branch, summed, doubled))
+        begin = end
+    return jnp.concatenate(outs, axis=1)
 
 
 def solution(mesh):

time: 213 us -> 217 us (1.019)
  the two profiles are of different devices: /device:TPU:178 before, /device:TPU:326 now
where the time goes in v4:
time: 217 us; the launch traced here: 216 us
  starting transfers between devices  130 us (60%)
  waiting for transfers between devices  47.8 us (22%)
  matrix products  19.7 us (9%)
  other arithmetic  9.06 us (4%)
  local copies, waits for them, and re-layouts  8.4 us (4%)
    ppermute x21, starting transfers between devices, move(): lax.ppermute(value, ('row', 'col'), [p for p in pairs if p[1] is not None])  123 us
    ppermute x21, waiting for transfers between devices, move(): lax.ppermute(value, ('row', 'col'), [p for p in pairs if p[1] is not None])  47.8 us
    dot_general x24, matrix products, contract(): lax.dot_general(a, b, (((1,), (1,)), ((), ())), preferred_element_type=jn...  17.6 us
    select_n x3, other arithmetic, body(): chosen = jnp.where(to <= low, *held)  5.46 us
  transfers between devices with their start and end apart: 24, of which 10 were waited for; matrix products, arithmetic and copies ran while one was open for 14% of the time, Pallas kernels for 0%

profile of v4, /device:TPU:326, one launch (start us, length us, event | category | flops | bytes accessed | tf_op | source)
XLA Modules:
  0.0 215.8 jit_solution(8331717638876544196)
XLA Ops:
  0.0 2.1 fusion
  2.8 5.1 %collective-permute-start.3 = (bf16[256,512]{0,1:T(8,128)(2,1)S(1)}, bf16[256,512]{0,1:T(8,128)(2,1)}, u32[]{:S(2)}, u32[]{:S(2)}) collective-permute-start(bf16[256,512]{0,1:T(8,128)(2,1)S(1)} %bitcast.107), channel_id=1, source_target_pairs={{0,0},{1,1},{2,2},{3,3},{4,128},{5,129},{6,130},{7,131},{8,256},{9... | collective-permute-start | bytes 786440 | tf_op jit(solution)/shard_map/ppermute | solution.py:26
  14.2 5.0 %collective-permute-done.3 = bf16[256,512]{0,1:T(8,128)(2,1)} collective-permute-done((bf16[256,512]{0,1:T(8,128)(2,1)S(1)}, bf16[256,512]{0,1:T(8,128)(2,1)}, u32[]{:S(2)}, u32[]{:S(2)}) %collective-permute-start.3) | collective-permute-done | bytes 262176 | tf_op jit(solution)/shard_map/ppermute | solution.py:26
  19.2 3.6 %collective-permute-done.4 = bf16[256,512]{0,1:T(8,128)(2,1)} collective-permute-done((bf16[256,512]{0,1:T(8,128)(2,1)S(1)}, bf16[256,512]{0,1:T(8,128)(2,1)}, u32[]{:S(2)}, u32[]{:S(2)}) %collective-permute-start.4) | collective-permute-done | bytes 262176 | tf_op jit(solution)/shard_map/ppermute | solution.py:26
  22.9 4.3 %collective-permute-start.6 = (bf16[384,512]{1,0:T(8,128)(2,1)}, bf16[384,512]{1,0:T(8,128)(2,1)}, u32[]{:S(2)}, u32[]{:S(2)}) collective-permute-start(bf16[384,512]{1,0:T(8,128)(2,1)} %get-tuple-element.26), channel_id=1, source_target_pairs={{0,0},{1,1},{2,2},{3,3},{4,128},{5,129},{6,130},{7,131},{8,256},{9... | collective-permute-start | bytes 1179656 | tf_op jit(solution)/shard_map/ppermute | solution.py:26
  29.1 2.1 broadcast_select_fusion.11
  31.2 8.2 %collective-permute-start.5 = (bf16[256,512]{0,1:T(8,128)(2,1)}, bf16[256,512]{0,1:T(8,128)(2,1)S(1)}, u32[]{:S(2)}, u32[]{:S(2)}) collective-permute-start(bf16[256,512]{0,1:T(8,128)(2,1)} %get-tuple-element.59), channel_id=1, source_target_pairs={{0,0},{1,64},{2,32},{3,96},{4,4},{5,68},{6,36},{7,100},{8,8},{9,72... | collective-permute-start | bytes 786440 | tf_op jit(solution)/shard_map/ppermute | solution.py:26
  41.4 7.1 %collective-permute-done.5 = bf16[256,512]{0,1:T(8,128)(2,1)S(1)} collective-permute-done((bf16[256,512]{0,1:T(8,128)(2,1)}, bf16[256,512]{0,1:T(8,128)(2,1)S(1)}, u32[]{:S(2)}, u32[]{:S(2)}) %collective-permute-start.5) | collective-permute-done | bytes 262176 | tf_op jit(solution)/shard_map/ppermute | solution.py:26
  48.4 12.1 %collective-permute-start.9 = (bf16[256,512]{0,1:T(8,128)(2,1)}, bf16[256,512]{0,1:T(8,128)(2,1)S(1)}, u32[]{:S(2)}, u32[]{:S(2)}) collective-permute-start(bf16[256,512]{0,1:T(8,128)(2,1)} %get-tuple-element.60), channel_id=1, source_target_pairs={{0,64},{1,0},{2,96},{3,32},{4,68},{5,4},{6,100},{7,36},{8,72},{9,8... | collective-permute-start | bytes 786440 | tf_op jit(solution)/shard_map/ppermute | solution.py:26
  60.6 17.7 %collective-permute-start.10 = (bf16[256,512]{0,1:T(8,128)(2,1)}, bf16[256,512]{0,1:T(8,128)(2,1)S(1)}, u32[]{:S(2)}, u32[]{:S(2)}) collective-permute-start(bf16[256,512]{0,1:T(8,128)(2,1)} %get-tuple-element.29), channel_id=1, source_target_pairs={{0,96},{1,32},{2,64},{3,0},{4,100},{5,36},{6,68},{7,4},{8,104},{9,... | collective-permute-start | bytes 786440 | tf_op jit(solution)/shard_map/ppermute | solution.py:26
  80.3 2.1 broadcast_select_fusion.4
  84.4 5.8 %collective-permute-start.12 = (bf16[384,512]{1,0:T(8,128)(2,1)S(1)}, bf16[384,512]{1,0:T(8,128)(2,1)}, u32[]{:S(2)}, u32[]{:S(2)}) collective-permute-start(bf16[384,512]{1,0:T(8,128)(2,1)S(1)} %get-tuple-element.31), channel_id=1, source_target_pairs={{0,0},{1,64},{2,32},{3,96},{4,4},{5,68},{6,36},{7,100},{8,8},{9,72... | collective-permute-start | bytes 1179656 | tf_op jit(solution)/shard_map/ppermute | solution.py:26
  91.3 3.2 %collective-permute-start.1 = (bf16[1024,512]{1,0:T(8,128)(2,1)}, bf16[1024,512]{1,0:T(8,128)(2,1)}, u32[]{:S(2)}, u32[]{:S(2)}) collective-permute-start(bf16[1024,512]{1,0:T(8,128)(2,1)} %broadcast_select_fusion), channel_id=1, source_target_pairs={{0,15},{1,0},{2,1},{3,2},{4,3},{5,4},{6,5},{7,6},{8,7},{9,8},{10,9... | collective-permute-start | bytes 3145736 | tf_op jit(solution)/shard_map/ppermute | solution.py:88
  96.5 6.0 %collective-permute-done.12 = bf16[384,512]{1,0:T(8,128)(2,1)} collective-permute-done((bf16[384,512]{1,0:T(8,128)(2,1)S(1)}, bf16[384,512]{1,0:T(8,128)(2,1)}, u32[]{:S(2)}, u32[]{:S(2)}) %collective-permute-start.12) | collective-permute-done | bytes 393248 | tf_op jit(solution)/shard_map/ppermute | solution.py:26
  104.4 3.6 %collective-permute-start.16 = (bf16[384,512]{1,0:T(8,128)(2,1)}, bf16[384,512]{1,0:T(8,128)(2,1)}, u32[]{:S(2)}, u32[]{:S(2)}) collective-permute-start(bf16[384,512]{1,0:T(8,128)(2,1)} %get-tuple-element.36), channel_id=1, source_target_pairs={{0,64},{1,0},{2,96},{3,32},{4,68},{5,4},{6,100},{7,36},{8,72},{9,8... | collective-permute-start | bytes 1179656 | tf_op jit(solution)/shard_map/ppermute | solution.py:26
  108.0 7.1 %collective-permute-start.17 = (bf16[384,512]{1,0:T(8,128)(2,1)}, bf16[384,512]{1,0:T(8,128)(2,1)}, u32[]{:S(2)}, u32[]{:S(2)}) collective-permute-start(bf16[384,512]{1,0:T(8,128)(2,1)} %get-tuple-element.38), channel_id=1, source_target_pairs={{0,96},{1,32},{2,64},{3,0},{4,100},{5,36},{6,68},{7,4},{8,104},{9,... | collective-permute-start | bytes 1179656 | tf_op jit(solution)/shard_map/ppermute | solution.py:26
  116.6 3.4 %collective-permute-start.19 = (bf16[384,512]{1,0:T(8,128)(2,1)}, bf16[384,512]{1,0:T(8,128)(2,1)}, u32[]{:S(2)}, u32[]{:S(2)}) collective-permute-start(bf16[384,512]{1,0:T(8,128)(2,1)} %get-tuple-element.40), channel_id=1, source_target_pairs={{0,0},{1,64},{2,32},{3,96},{4,4},{5,68},{6,36},{7,100},{8,8},{9,72... | collective-permute-start | bytes 1179656 | tf_op jit(solution)/shard_map/ppermute | solution.py:26
  123.7 5.5 %collective-permute-done.16 = bf16[384,512]{1,0:T(8,128)(2,1)} collective-permute-done((bf16[384,512]{1,0:T(8,128)(2,1)}, bf16[384,512]{1,0:T(8,128)(2,1)}, u32[]{:S(2)}, u32[]{:S(2)}) %collective-permute-start.16) | collective-permute-done | bytes 393248 | tf_op jit(solution)/shard_map/ppermute | solution.py:26
  131.1 2.3 %collective-permute-done.17 = bf16[384,512]{1,0:T(8,128)(2,1)} collective-permute-done((bf16[384,512]{1,0:T(8,128)(2,1)}, bf16[384,512]{1,0:T(8,128)(2,1)}, u32[]{:S(2)}, u32[]{:S(2)}) %collective-permute-start.17) | collective-permute-done | bytes 393248 | tf_op jit(solution)/shard_map/ppermute | solution.py:26
  135.3 12.5 %collective-permute-done.19 = bf16[384,512]{1,0:T(8,128)(2,1)} collective-permute-done((bf16[384,512]{1,0:T(8,128)(2,1)}, bf16[384,512]{1,0:T(8,128)(2,1)}, u32[]{:S(2)}, u32[]{:S(2)}) %collective-permute-start.19) | collective-permute-done | bytes 393248 | tf_op jit(solution)/shard_map/ppermute | solution.py:26
  147.8 5.3 %collective-permute-start.22 = (bf16[384,512]{1,0:T(8,128)(2,1)}, bf16[384,512]{1,0:T(8,128)(2,1)S(1)}, u32[]{:S(2)}, u32[]{:S(2)}) collective-permute-start(bf16[384,512]{1,0:T(8,128)(2,1)} %get-tuple-element.44), channel_id=1, source_target_pairs={{0,96},{1,32},{2,64},{3,0},{4,100},{5,36},{6,68},{7,4},{8,104},{9,... | collective-permute-start | bytes 1179656 | tf_op jit(solution)/shard_map/ppermute | solution.py:26
  157.2 28.6 %collective-permute-start.11 = (f16[512,256]{0,1:T(8,128)(2,1)S(1)}, f16[512,256]{0,1:T(8,128)(2,1)S(1)}, u32[]{:S(2)}, u32[]{:S(2)}) collective-permute-start(f16[512,256]{0,1:T(8,128)(2,1)S(1)} %fusion.18), channel_id=1, source_target_pairs={{0,16},{1,17},{2,18},{3,19},{4,20},{5,21},{6,22},{7,23},{8,24},{9,... | collective-permute-start | bytes 786440 | tf_op jit(solution)/shard_map/ppermute | solution.py:26
  198.6 4.2 %collective-permute-start.23 = (f16[512,384]{0,1:T(8,128)(2,1)S(1)}, f16[512,384]{0,1:T(8,128)(2,1)S(1)}, u32[]{:S(2)}, u32[]{:S(2)}) collective-permute-start(f16[512,384]{0,1:T(8,128)(2,1)S(1)} %fusion.11), channel_id=1, source_target_pairs={{0,16},{1,17},{2,18},{3,19},{4,20},{5,21},{6,22},{7,23},{8,24},{9,... | collective-permute-start | bytes 1179656 | tf_op jit(solution)/shard_map/ppermute | solution.py:26
  207.0 5.3 %collective-permute-done.23 = f16[512,384]{0,1:T(8,128)(2,1)S(1)} collective-permute-done((f16[512,384]{0,1:T(8,128)(2,1)S(1)}, f16[512,384]{0,1:T(8,128)(2,1)S(1)}, u32[]{:S(2)}, u32[]{:S(2)}) %collective-permute-start.23) | collective-permute-done | bytes 393248 | tf_op jit(solution)/shard_map/ppermute | solution.py:26
  (97 shorter events, 52.4 us)
Async XLA Ops:
  2.8 16.4 %collective-permute-start.3 = (bf16[256,512]{0,1:T(8,128)(2,1)S(1)}, bf16[256,512]{0,1:T(8,128)(2,1)}, u32[]{:S(2)}, u32[]{:S(2)}) collective-permute-start(bf16[256,512]{0,1:T(8,128)(2,1)S(1)} %bitcast.107), channel_id=1, source_target_pairs={{0,0},{1,1},{2,2},{3,3},{4,128},{5,129},{6,130},{7,131},{8,256},{9... | collective-permute-start | bytes 786440 | tf_op jit(solution)/shard_map/ppermute | solution.py:26
  8.0 14.9 %collective-permute-start.4 = (bf16[256,512]{0,1:T(8,128)(2,1)S(1)}, bf16[256,512]{0,1:T(8,128)(2,1)}, u32[]{:S(2)}, u32[]{:S(2)}) collective-permute-start(bf16[256,512]{0,1:T(8,128)(2,1)S(1)} %bitcast.108), channel_id=1, source_target_pairs={{0,384},{1,385},{2,386},{4,0},{5,1},{6,2},{8,128},{9,129},{10,130}... | collective-permute-start | bytes 786440 | tf_op jit(solution)/shard_map/ppermute | solution.py:26
  11.2 73.1 %collective-permute-start = (bf16[1024,512]{1,0:T(8,128)(2,1)S(1)}, bf16[1024,512]{1,0:T(8,128)(2,1)S(1)}, u32[]{:S(2)}, u32[]{:S(2)}) collective-permute-start(bf16[1024,512]{1,0:T(8,128)(2,1)S(1)} %bitcast.102), channel_id=1, source_target_pairs={{0,14},{1,15},{2,0},{3,1},{4,2},{5,3},{6,4},{7,5},{8,6},{9,7},{10,... | collective-permute-start | bytes 3145736 | tf_op jit(solution)/shard_map/ppermute | solution.py:86
  22.9 37.7 %collective-permute-start.6 = (bf16[384,512]{1,0:T(8,128)(2,1)}, bf16[384,512]{1,0:T(8,128)(2,1)}, u32[]{:S(2)}, u32[]{:S(2)}) collective-permute-start(bf16[384,512]{1,0:T(8,128)(2,1)} %get-tuple-element.26), channel_id=1, source_target_pairs={{0,0},{1,1},{2,2},{3,3},{4,128},{5,129},{6,130},{7,131},{8,256},{9... | collective-permute-start | bytes 1179656 | tf_op jit(solution)/shard_map/ppermute | solution.py:26
  27.2 51.1 %collective-permute-start.7 = (bf16[384,512]{1,0:T(8,128)(2,1)}, bf16[384,512]{1,0:T(8,128)(2,1)}, u32[]{:S(2)}, u32[]{:S(2)}) collective-permute-start(bf16[384,512]{1,0:T(8,128)(2,1)} %get-tuple-element.26), channel_id=1, source_target_pairs={{0,384},{1,385},{2,386},{4,0},{5,1},{6,2},{8,128},{9,129},{10,130}... | collective-permute-start | bytes 1179656 | tf_op jit(solution)/shard_map/ppermute | solution.py:26
  31.2 17.2 %collective-permute-start.5 = (bf16[256,512]{0,1:T(8,128)(2,1)}, bf16[256,512]{0,1:T(8,128)(2,1)S(1)}, u32[]{:S(2)}, u32[]{:S(2)}) collective-permute-start(bf16[256,512]{0,1:T(8,128)(2,1)} %get-tuple-element.59), channel_id=1, source_target_pairs={{0,0},{1,64},{2,32},{3,96},{4,4},{5,68},{6,36},{7,100},{8,8},{9,72... | collective-permute-start | bytes 786440 | tf_op jit(solution)/shard_map/ppermute | solution.py:26
  39.4 43.0 %collective-permute-start.8 = (bf16[256,512]{0,1:T(8,128)(2,1)}, bf16[256,512]{0,1:T(8,128)(2,1)S(1)}, u32[]{:S(2)}, u32[]{:S(2)}) collective-permute-start(bf16[256,512]{0,1:T(8,128)(2,1)} %get-tuple-element.61), channel_id=1, source_target_pairs={{0,32},{1,96},{2,0},{3,64},{4,36},{5,100},{6,4},{7,68},{8,40},{9,1... | collective-permute-start | bytes 786440 | tf_op jit(solution)/shard_map/ppermute | solution.py:26
  48.4 42.9 %collective-permute-start.9 = (bf16[256,512]{0,1:T(8,128)(2,1)}, bf16[256,512]{0,1:T(8,128)(2,1)S(1)}, u32[]{:S(2)}, u32[]{:S(2)}) collective-permute-start(bf16[256,512]{0,1:T(8,128)(2,1)} %get-tuple-element.60), channel_id=1, source_target_pairs={{0,64},{1,0},{2,96},{3,32},{4,68},{5,4},{6,100},{7,36},{8,72},{9,8... | collective-permute-start | bytes 786440 | tf_op jit(solution)/shard_map/ppermute | solution.py:26
  60.6 34.0 %collective-permute-start.10 = (bf16[256,512]{0,1:T(8,128)(2,1)}, bf16[256,512]{0,1:T(8,128)(2,1)S(1)}, u32[]{:S(2)}, u32[]{:S(2)}) collective-permute-start(bf16[256,512]{0,1:T(8,128)(2,1)} %get-tuple-element.29), channel_id=1, source_target_pairs={{0,96},{1,32},{2,64},{3,0},{4,100},{5,36},{6,68},{7,4},{8,104},{9,... | collective-permute-start | bytes 786440 | tf_op jit(solution)/shard_map/ppermute | solution.py:26
  78.3 26.1 %collective-permute-start.13 = (bf16[384,512]{1,0:T(8,128)(2,1)}, bf16[384,512]{1,0:T(8,128)(2,1)S(1)}, u32[]{:S(2)}, u32[]{:S(2)}) collective-permute-start(bf16[384,512]{1,0:T(8,128)(2,1)} %get-tuple-element.33), channel_id=1, source_target_pairs={{0,0},{1,1},{2,2},{3,3},{4,128},{5,129},{6,130},{7,131},{8,256},{9... | collective-permute-start | bytes 1179656 | tf_op jit(solution)/shard_map/ppermute | solution.py:26
  82.4 25.6 %collective-permute-start.14 = (bf16[384,512]{1,0:T(8,128)(2,1)}, bf16[384,512]{1,0:T(8,128)(2,1)S(1)}, u32[]{:S(2)}, u32[]{:S(2)}) collective-permute-start(bf16[384,512]{1,0:T(8,128)(2,1)} %get-tuple-element.33), channel_id=1, source_target_pairs={{0,384},{1,385},{2,386},{4,0},{5,1},{6,2},{8,128},{9,129},{10,130}... | collective-permute-start | bytes 1179656 | tf_op jit(solution)/shard_map/ppermute | solution.py:26
  84.4 18.1 %collective-permute-start.12 = (bf16[384,512]{1,0:T(8,128)(2,1)S(1)}, bf16[384,512]{1,0:T(8,128)(2,1)}, u32[]{:S(2)}, u32[]{:S(2)}) collective-permute-start(bf16[384,512]{1,0:T(8,128)(2,1)S(1)} %get-tuple-element.31), channel_id=1, source_target_pairs={{0,0},{1,64},{2,32},{3,96},{4,4},{5,68},{6,36},{7,100},{8,8},{9,72... | collective-permute-start | bytes 1179656 | tf_op jit(solution)/shard_map/ppermute | solution.py:26
  91.3 61.8 %collective-permute-start.1 = (bf16[1024,512]{1,0:T(8,128)(2,1)}, bf16[1024,512]{1,0:T(8,128)(2,1)}, u32[]{:S(2)}, u32[]{:S(2)}) collective-permute-start(bf16[1024,512]{1,0:T(8,128)(2,1)} %broadcast_select_fusion), channel_id=1, source_target_pairs={{0,15},{1,0},{2,1},{3,2},{4,3},{5,4},{6,5},{7,6},{8,7},{9,8},{10,9... | collective-permute-start | bytes 3145736 | tf_op jit(solution)/shard_map/ppermute | solution.py:88
  94.5 58.5 %collective-permute-start.2 = (bf16[1024,512]{1,0:T(8,128)(2,1)S(1)}, bf16[1024,512]{1,0:T(8,128)(2,1)}, u32[]{:S(2)}, u32[]{:S(2)}) collective-permute-start(bf16[1024,512]{1,0:T(8,128)(2,1)S(1)} %collective-permute-done), channel_id=1, source_target_pairs={{0,1},{1,0},{2,3},{3,2},{4,5},{5,4},{6,7},{7,6},{8,9},{9,8},{10,11... | collective-permute-start | bytes 3145736 | tf_op jit(solution)/shard_map/ppermute | solution.py:87
  102.5 14.1 %collective-permute-start.15 = (bf16[384,512]{1,0:T(8,128)(2,1)S(1)}, bf16[384,512]{1,0:T(8,128)(2,1)S(1)}, u32[]{:S(2)}, u32[]{:S(2)}) collective-permute-start(bf16[384,512]{1,0:T(8,128)(2,1)S(1)} %get-tuple-element.34), channel_id=1, source_target_pairs={{0,32},{1,96},{2,0},{3,64},{4,36},{5,100},{6,4},{7,68},{8,40},{9,1... | collective-permute-start | bytes 1179656 | tf_op jit(solution)/shard_map/ppermute | solution.py:26
  104.4 24.8 %collective-permute-start.16 = (bf16[384,512]{1,0:T(8,128)(2,1)}, bf16[384,512]{1,0:T(8,128)(2,1)}, u32[]{:S(2)}, u32[]{:S(2)}) collective-permute-start(bf16[384,512]{1,0:T(8,128)(2,1)} %get-tuple-element.36), channel_id=1, source_target_pairs={{0,64},{1,0},{2,96},{3,32},{4,68},{5,4},{6,100},{7,36},{8,72},{9,8... | collective-permute-start | bytes 1179656 | tf_op jit(solution)/shard_map/ppermute | solution.py:26
  108.0 25.4 %collective-permute-start.17 = (bf16[384,512]{1,0:T(8,128)(2,1)}, bf16[384,512]{1,0:T(8,128)(2,1)}, u32[]{:S(2)}, u32[]{:S(2)}) collective-permute-start(bf16[384,512]{1,0:T(8,128)(2,1)} %get-tuple-element.38), channel_id=1, source_target_pairs={{0,96},{1,32},{2,64},{3,0},{4,100},{5,36},{6,68},{7,4},{8,104},{9,... | collective-permute-start | bytes 1179656 | tf_op jit(solution)/shard_map/ppermute | solution.py:26
  116.6 31.2 %collective-permute-start.19 = (bf16[384,512]{1,0:T(8,128)(2,1)}, bf16[384,512]{1,0:T(8,128)(2,1)}, u32[]{:S(2)}, u32[]{:S(2)}) collective-permute-start(bf16[384,512]{1,0:T(8,128)(2,1)} %get-tuple-element.40), channel_id=1, source_target_pairs={{0,0},{1,64},{2,32},{3,96},{4,4},{5,68},{6,36},{7,100},{8,8},{9,72... | collective-permute-start | bytes 1179656 | tf_op jit(solution)/shard_map/ppermute | solution.py:26
  129.2 66.4 %collective-permute-start.20 = (bf16[384,512]{1,0:T(8,128)(2,1)}, bf16[384,512]{1,0:T(8,128)(2,1)S(1)}, u32[]{:S(2)}, u32[]{:S(2)}) collective-permute-start(bf16[384,512]{1,0:T(8,128)(2,1)} %get-tuple-element.42), channel_id=1, source_target_pairs={{0,32},{1,96},{2,0},{3,64},{4,36},{5,100},{6,4},{7,68},{8,40},{9,1... | collective-permute-start | bytes 1179656 | tf_op jit(solution)/shard_map/ppermute | solution.py:26
  133.4 63.0 %collective-permute-start.21 = (bf16[384,512]{1,0:T(8,128)(2,1)}, bf16[384,512]{1,0:T(8,128)(2,1)S(1)}, u32[]{:S(2)}, u32[]{:S(2)}) collective-permute-start(bf16[384,512]{1,0:T(8,128)(2,1)} %get-tuple-element.43), channel_id=1, source_target_pairs={{0,64},{1,0},{2,96},{3,32},{4,68},{5,4},{6,100},{7,36},{8,72},{9,8... | collective-permute-start | bytes 1179656 | tf_op jit(solution)/shard_map/ppermute | solution.py:26
  147.8 49.0 %collective-permute-start.22 = (bf16[384,512]{1,0:T(8,128)(2,1)}, bf16[384,512]{1,0:T(8,128)(2,1)S(1)}, u32[]{:S(2)}, u32[]{:S(2)}) collective-permute-start(bf16[384,512]{1,0:T(8,128)(2,1)} %get-tuple-element.44), channel_id=1, source_target_pairs={{0,96},{1,32},{2,64},{3,0},{4,100},{5,36},{6,68},{7,4},{8,104},{9,... | collective-permute-start | bytes 1179656 | tf_op jit(solution)/shard_map/ppermute | solution.py:26
  157.2 47.6 %collective-permute-start.11 = (f16[512,256]{0,1:T(8,128)(2,1)S(1)}, f16[512,256]{0,1:T(8,128)(2,1)S(1)}, u32[]{:S(2)}, u32[]{:S(2)}) collective-permute-start(f16[512,256]{0,1:T(8,128)(2,1)S(1)} %fusion.18), channel_id=1, source_target_pairs={{0,16},{1,17},{2,18},{3,19},{4,20},{5,21},{6,22},{7,23},{8,24},{9,... | collective-permute-start | bytes 786440 | tf_op jit(solution)/shard_map/ppermute | solution.py:26
  190.4 15.0 %collective-permute-start.18 = (f16[512,384]{0,1:T(8,128)(2,1)S(1)}, f16[512,384]{0,1:T(8,128)(2,1)S(1)}, u32[]{:S(2)}, u32[]{:S(2)}) collective-permute-start(f16[512,384]{0,1:T(8,128)(2,1)S(1)} %fusion.12), channel_id=1, source_target_pairs={{0,16},{1,17},{2,18},{3,19},{4,20},{5,21},{6,22},{7,23},{8,24},{9,... | collective-permute-start | bytes 1179656 | tf_op jit(solution)/shard_map/ppermute | solution.py:26
  198.6 13.7 %collective-permute-start.23 = (f16[512,384]{0,1:T(8,128)(2,1)S(1)}, f16[512,384]{0,1:T(8,128)(2,1)S(1)}, u32[]{:S(2)}, u32[]{:S(2)}) collective-permute-start(f16[512,384]{0,1:T(8,128)(2,1)S(1)} %fusion.11), channel_id=1, source_target_pairs={{0,16},{1,17},{2,18},{3,19},{4,20},{5,21},{6,22},{7,23},{8,24},{9,... | collective-permute-start | bytes 1179656 | tf_op jit(solution)/shard_map/ppermute | solution.py:26
  (13 other events, 206.4 us)
